TPU v7x, 128 devices: a whole 4x4x4 slice. The times are simulated.
128 devices in a mesh: head: 4 (over y), dp: 32 (over x, z, core).
Axes of the slice: x: 4, y: 4, z: 4, core: 2. Of those that a mesh axis runs over, the one named last changes fastest.
Arguments:
- tokens: bfloat16 [32, 1024, 768], P('dp', 'head'), may hold values from -6 to 6
- lengths: int32 [32], P('dp'), may hold values from 64 to 1024, as said below
- cotangent: bfloat16 [32, 1024, 768], P('dp', 'head'), may hold values from -6 to 6
- gains: float32 [2, 768], replicated, may hold values from 0.2 to 5.1
- conv: float32 [3, 3, 768], replicated, may hold values from -3.6 to 3.6
- w_qkv: float32 [3, 768, 768], P(None, 'dp', 'head'), may hold values from -0.21875 to 0.21875
- w_out: float32 [768, 768], P('head', 'dp'), may hold values from -2.0412415 to 2.0412415
- ffn_weights: float32 [2, 3072, 768], P(None, ('head', 'dp')), may hold values from -0.36084392 to 0.36084392
- mom_qkv: float32 [3, 768, 768], P(None, 'dp', 'head'), may hold values from -0.005859375 to 0.005859375
- mom_out: float32 [768, 768], P('head', 'dp'), may hold values from -0.005859375 to 0.005859375
- mom_ffn: float32 [2, 3072, 768], P(None, ('head', 'dp')), may hold values from -0.005859375 to 0.005859375
- gain_first: float32 [2, 768], replicated, may hold values from -0.001953125 to 0.001953125
- gain_second: float32 [2, 768], replicated, may hold values from 1.2715657e-09 to 5.086263e-09
- conv_first: float32 [3, 3, 768], replicated, may hold values from -0.001953125 to 0.001953125
- conv_second: float32 [3, 3, 768], replicated, may hold values from 1.2715657e-09 to 5.086263e-09
Outputs:
- output: float32 [32, 1024, 768], P('dp', 'head')
- input_grad: float32 [32, 1024, 768], P('dp', 'head')
- grad_gains: float32 [2, 768], replicated
- grad_conv: float32 [3, 3, 768], replicated
- grad_qkv: float32 [3, 768, 768], P(None, 'dp', 'head')
- grad_out: float32 [768, 768], P('head', 'dp')
- grad_ffn: float32 [2, 3072, 768], P(None, ('head', 'dp'))
- grad_norm: float32 [], replicated
- new_mom_qkv: float32 [3, 768, 768], P(None, 'dp', 'head')
- new_mom_out: float32 [768, 768], P('head', 'dp')
- new_mom_ffn: float32 [2, 3072, 768], P(None, ('head', 'dp'))
- new_gain_first: float32 [2, 768], replicated
- new_gain_second: float32 [2, 768], replicated
- new_conv_first: float32 [3, 3, 768], replicated
- new_conv_second: float32 [3, 3, 768], replicated
- new_gains: float32 [2, 768], replicated
- new_conv: float32 [3, 3, 768], replicated
- new_qkv: float32 [3, 768, 768], P(None, 'dp', 'head')
- new_out: float32 [768, 768], P('head', 'dp')
- new_ffn: float32 [2, 3072, 768], P(None, ('head', 'dp'))
Inputs may be any that keep to these rules, and one draw needn't show every extreme that they name: Sequence s has real tokens at positions below lengths[s]; one of the last 1 sequence has exactly 1024.
All inputs are finite; a program needn't handle non-finite values.
Results may differ from a plain program's by a relative error of at most 0.023.
The roundings to bfloat16 on the way count: a program that leaves them out, or rounds other values in their place, can miss the bound.
Values may be sent and summed in bfloat16 or wider, within the bound.
A program may use at most 128 MiB of HBM per device.

v0:
```python
import math

import jax
import jax.numpy as jnp
from jax import lax
from jax.sharding import PartitionSpec as P

D = 768
HEADS = 12
HEAD_DIM = 64
FF = 3072
KW = 3
NS_ITERS = 5
STEP = 10


NORM_EPS = 1e-06
NEG_FILL = -1e30
CLIP_NORM = 1.0
MOMENTUM = 0.95
RATE_IN = 0.02
RATE_OUT = 0.15
ADAM_RATE = 0.5
BETA_ONE = 0.9
BETA_TWO = 0.999
ADAM_EPS = 1e-08
NS_EPS = 1e-07
COEF_A = 3.4445
COEF_B = -4.775
COEF_C = 2.0315
PRECISE = lax.Precision.HIGHEST


def norm_parts(values, gain):
    inverse = lax.rsqrt(jnp.mean(values * values, axis=-1, keepdims=True) + NORM_EPS)
    unit_rows = values * inverse
    return (unit_rows, inverse, (unit_rows * gain).astype(jnp.bfloat16))


def norm_back(upstream, unit_rows, inverse, gain):
    scaled = upstream * gain
    centred = scaled - unit_rows * jnp.mean(scaled * unit_rows, axis=-1, keepdims=True)
    return (inverse * centred, jnp.sum(upstream * unit_rows, axis=(0, 1)))


def shift_down(values, offset):
    return jnp.pad(values, ((0, 0), (0, 0), (offset, 0), (0, 0)))[:, :, : values.shape[2]]


def shift_up(values, offset):
    return jnp.pad(values, ((0, 0), (0, 0), (0, offset), (0, 0)))[:, :, offset:]


def conv_forward(projected_rows, kernel):
    summed = kernel[0][:, None, None, :] * projected_rows
    for offset in range(1, KW):
        summed = summed + kernel[offset][:, None, None, :] * shift_down(projected_rows, offset)
    return summed


def conv_back(upstream_lower_rows, projected_rows, kernel):
    upstream = upstream_lower_rows.astype(jnp.float32)
    summed = kernel[0][:, None, None, :] * upstream
    pieces = [jnp.sum(upstream * projected_rows, axis=(1, 2))]
    for offset in range(1, KW):
        summed = summed + kernel[offset][:, None, None, :] * shift_up(upstream, offset)
        pieces.append(jnp.sum(upstream * shift_down(projected_rows, offset), axis=(1, 2)))
    return (summed, jnp.stack(pieces))


def masked_scores(query_rows, keys_all, start_row, length):
    raw_scores = jnp.einsum(
        "qhd,khd->hqk", query_rows, keys_all, preferred_element_type=jnp.float32
    )
    row_ids = start_row + jnp.arange(query_rows.shape[0])
    col_ids = jnp.arange(keys_all.shape[0])
    allowed = (col_ids[None, :] <= row_ids[:, None]) & (col_ids[None, :] < length)
    return jnp.where(allowed[None], raw_scores * HEAD_DIM ** (-0.5), NEG_FILL)


def attend_forward(queries, keys_all, values_all, length):
    seq_count = queries.shape[0]
    block_rows = min(512, seq_count)
    outputs, maxima, totals = ([], [], [])
    for start_row in range(0, seq_count, block_rows):
        scores = masked_scores(
            queries[start_row : start_row + block_rows], keys_all, start_row, length
        )
        row_max = jnp.max(scores, axis=-1, keepdims=True)
        lifted = jnp.exp(scores - row_max)
        row_sum = jnp.sum(lifted, axis=-1, keepdims=True)
        weight_collection = (lifted / row_sum).astype(jnp.bfloat16)
        outputs.append(
            jnp.einsum(
                "hqk,khd->qhd", weight_collection, values_all, preferred_element_type=jnp.float32
            )
        )
        maxima.append(row_max)
        totals.append(row_sum)
    return (jnp.concatenate(outputs, 0), jnp.concatenate(maxima, 1), jnp.concatenate(totals, 1))


def attend_back(queries, keys_all, values_all, length, maxima, totals, upstream):
    seq_count = queries.shape[0]
    block_rows = min(512, seq_count)
    query_grads = []
    key_grad = jnp.zeros(keys_all.shape, jnp.float32)
    value_grad = jnp.zeros(values_all.shape, jnp.float32)
    for start_row in range(0, seq_count, block_rows):
        stop_row = start_row + block_rows
        query_rows = queries[start_row:stop_row]
        upstream_rows = upstream[start_row:stop_row]
        scores = masked_scores(query_rows, keys_all, start_row, length)
        probs_full = jnp.exp(scores - maxima[:, start_row:stop_row]) / totals[:, start_row:stop_row]
        prob_grad = jnp.einsum(
            "qhd,khd->hqk", upstream_rows, values_all, preferred_element_type=jnp.float32
        )
        centre = jnp.sum(prob_grad * probs_full, axis=-1, keepdims=True)
        score_grad = (probs_full * (prob_grad - centre) * HEAD_DIM ** (-0.5)).astype(jnp.bfloat16)
        query_grads.append(
            jnp.einsum("hqk,khd->qhd", score_grad, keys_all, preferred_element_type=jnp.float32)
        )
        key_grad = key_grad + jnp.einsum(
            "hqk,qhd->khd", score_grad, query_rows, preferred_element_type=jnp.float32
        )
        value_grad = value_grad + jnp.einsum(
            "hqk,qhd->khd",
            probs_full.astype(jnp.bfloat16),
            upstream_rows,
            preferred_element_type=jnp.float32,
        )
    return (jnp.concatenate(query_grads, 0), key_grad, value_grad)


def ffn_forward(normalized_rows, weight_collection):
    hidden_state_rows = jnp.einsum(
        "cbv,jv->cbj", normalized_rows, weight_collection[0], preferred_element_type=jnp.float32
    )
    relu_active_rows = jnp.square(jnp.maximum(hidden_state_rows, 0.0)).astype(jnp.bfloat16)
    return (
        hidden_state_rows,
        relu_active_rows,
        jnp.einsum(
            "gen,nc->gec",
            relu_active_rows,
            weight_collection[1],
            preferred_element_type=jnp.float32,
        ),
    )


def ffn_back(
    normalized_rows, weight_collection, hidden_state_rows, relu_active_rows, upstream_lower_rows
):
    grad_back_w = jnp.einsum(
        "vgq,vgh->qh", relu_active_rows, upstream_lower_rows, preferred_element_type=jnp.float32
    )
    grad_active = jnp.einsum(
        "cbv,jv->cbj", upstream_lower_rows, weight_collection[1], preferred_element_type=jnp.float32
    )
    hidden_state_gradient = (grad_active * 2.0 * jnp.maximum(hidden_state_rows, 0.0)).astype(
        jnp.bfloat16
    )
    input_weight_gradient = jnp.einsum(
        "vgq,vgh->qh", hidden_state_gradient, normalized_rows, preferred_element_type=jnp.float32
    )
    grad_normed = jnp.einsum(
        "gen,nc->gec",
        hidden_state_gradient,
        weight_collection[0],
        preferred_element_type=jnp.float32,
    )
    return (grad_normed, jnp.stack([input_weight_gradient, grad_back_w]))


def ns_update(iterate, gram_matrix):
    polynomial = COEF_B * gram_matrix + COEF_C * jnp.einsum(
        "...de,...ef->...df", gram_matrix, gram_matrix, precision=PRECISE
    )
    return COEF_A * iterate + jnp.einsum(
        "...nd,...de->...ne", iterate, polynomial, precision=PRECISE
    )


def adam_step(weight, gradient, moment_one, moment_two):
    first_new = BETA_ONE * moment_one + (1.0 - BETA_ONE) * gradient
    second_new = BETA_TWO * moment_two + (1.0 - BETA_TWO) * gradient * gradient
    stepped = (
        first_new
        / (1.0 - BETA_ONE**STEP)
        / (jnp.sqrt(second_new / (1.0 - BETA_TWO**STEP)) + ADAM_EPS)
    )
    return (first_new, second_new, weight - ADAM_RATE * stepped)


def per_device(
    tokens,
    lengths,
    cotangent,
    gains,
    conv,
    w_qkv,
    w_out,
    ffn_weights,
    mom_qkv,
    mom_out,
    mom_ffn,
    gain_first,
    gain_second,
    conv_first,
    conv_second,
):
    heads_axis = lax.axis_size("head")
    head_at = lax.axis_index("head")
    seq_here, rows_here, width = tokens.shape
    seq_length = rows_here * heads_axis
    cols_here = w_qkv.shape[2]
    heads_local = cols_here // HEAD_DIM
    positions = head_at * rows_here + jnp.arange(rows_here)
    real_rows = (positions[None, :] < lengths[:, None]).astype(jnp.float32)[:, :, None]
    kernel = lax.dynamic_slice_in_dim(conv, head_at * cols_here, cols_here, 2)
    query_key_value_lower, output_lower_rows, ffn_low = (
        lax.all_gather(w_qkv.astype(jnp.bfloat16), "dp", axis=1, tiled=True),
        lax.all_gather(w_out.astype(jnp.bfloat16), "dp", axis=1, tiled=True),
        lax.all_gather(ffn_weights.astype(jnp.bfloat16), "dp", axis=1, tiled=True),
    )
    resid_in = tokens.astype(jnp.float32)
    unit_one, inverse_one, normed_one = norm_parts(resid_in, gains[0])
    normalized_every_row = lax.all_gather(normed_one, "head", axis=1, tiled=True)
    projected_rows = jnp.einsum(
        "vru,jua->jvra",
        normalized_every_row,
        query_key_value_lower,
        preferred_element_type=jnp.float32,
    )
    streams = conv_forward(projected_rows, kernel).astype(jnp.bfloat16)
    shaped = streams.reshape(3, seq_here, seq_length, heads_local, HEAD_DIM)

    def forward_one(bundle):
        return attend_forward(bundle[0], bundle[1], bundle[2], bundle[3])

    attended, maxima, totals = lax.map(forward_one, (shaped[0], shaped[1], shaped[2], lengths))
    attended_lower_rows = attended.reshape(seq_here, seq_length, cols_here).astype(jnp.bfloat16)
    projection_portion = jnp.einsum(
        "azp,pm->azm", attended_lower_rows, output_lower_rows, preferred_element_type=jnp.float32
    )
    attn_rows = lax.psum_scatter(projection_portion, "head", scatter_dimension=1, tiled=True)
    middle = resid_in + attn_rows
    unit_two, inverse_two, normed_two = norm_parts(middle, gains[1])
    upstream = cotangent.astype(jnp.float32) * real_rows
    upstream_lower_rows = upstream.astype(jnp.bfloat16)
    normed_wide = lax.all_gather(normed_two, "head", axis=1, tiled=True)
    hidden_state_rows, relu_active_rows, ffn_part = ffn_forward(normed_wide, ffn_low)
    ffn_rows_out = lax.psum_scatter(
        ffn_part.astype(jnp.bfloat16), "head", scatter_dimension=1, tiled=True
    ).astype(jnp.float32)
    output = middle + ffn_rows_out
    upstream_wide = lax.all_gather(upstream_lower_rows, "head", axis=1, tiled=True)
    grad_normed_part, ffn_grad = ffn_back(
        normed_wide, ffn_low, hidden_state_rows, relu_active_rows, upstream_wide
    )
    grad_normed_two = lax.psum_scatter(grad_normed_part, "head", scatter_dimension=1, tiled=True)
    grad_norm_two, gain_two_grad = norm_back(grad_normed_two, unit_two, inverse_two, gains[1])
    grad_middle = upstream + grad_norm_two
    attention_wide_gradient = lax.all_gather(
        grad_middle.astype(jnp.bfloat16), "head", axis=1, tiled=True
    )
    out_grad = jnp.einsum(
        "tzu,tzx->ux",
        attended_lower_rows,
        attention_wide_gradient,
        preferred_element_type=jnp.float32,
    )
    grad_attended = jnp.einsum(
        "kmh,uh->kmu",
        attention_wide_gradient,
        output_lower_rows,
        preferred_element_type=jnp.float32,
    ).astype(jnp.bfloat16)
    grad_shaped = grad_attended.reshape(seq_here, seq_length, heads_local, HEAD_DIM)

    def back_one(bundle):
        return attend_back(
            bundle[0], bundle[1], bundle[2], bundle[3], bundle[4], bundle[5], bundle[6]
        )

    query_grad, key_grad, value_grad = lax.map(
        back_one, (shaped[0], shaped[1], shaped[2], lengths, maxima, totals, grad_shaped)
    )
    grad_streams = (
        jnp.stack([query_grad, key_grad, value_grad])
        .reshape(3, seq_here, seq_length, cols_here)
        .astype(jnp.bfloat16)
    )
    grad_projected, kernel_grad = conv_back(grad_streams, projected_rows, kernel)
    projected_lower_gradient = grad_projected.astype(jnp.bfloat16)
    qkv_grad = jnp.einsum(
        "uvm,buvh->bmh",
        normalized_every_row,
        projected_lower_gradient,
        preferred_element_type=jnp.float32,
    )
    grad_normed_part_one = jnp.einsum(
        "rptv,rov->pto",
        projected_lower_gradient,
        query_key_value_lower,
        preferred_element_type=jnp.float32,
    )
    grad_normed_one = lax.psum_scatter(
        grad_normed_part_one.astype(jnp.bfloat16), "head", scatter_dimension=1, tiled=True
    ).astype(jnp.float32)
    grad_norm_one, gain_one_grad = norm_back(grad_normed_one, unit_one, inverse_one, gains[0])
    input_grad = grad_middle + grad_norm_one
    qkv_part, out_part, ffn_part_grad = (
        lax.psum_scatter(
            qkv_grad.astype(jnp.bfloat16), "dp", scatter_dimension=1, tiled=True
        ).astype(jnp.float32),
        lax.psum_scatter(
            out_grad.astype(jnp.bfloat16), "dp", scatter_dimension=1, tiled=True
        ).astype(jnp.float32),
        lax.psum_scatter(
            ffn_grad.astype(jnp.bfloat16), "dp", scatter_dimension=1, tiled=True
        ).astype(jnp.float32),
    )
    conv_placed = lax.dynamic_update_slice_in_dim(
        jnp.zeros(conv.shape, jnp.float32), kernel_grad, head_at * cols_here, 2
    )
    squares = (
        jnp.sum(qkv_part * qkv_part)
        + jnp.sum(out_part * out_part)
        + jnp.sum(ffn_part_grad * ffn_part_grad)
    )
    gain_sum, conv_sum, square_sum = lax.psum(
        (jnp.stack([gain_one_grad, gain_two_grad]), conv_placed, squares), ("head", "dp")
    )
    grad_norm = jnp.sqrt(square_sum + jnp.sum(gain_sum * gain_sum) + jnp.sum(conv_sum * conv_sum))
    factor = CLIP_NORM / jnp.maximum(grad_norm, CLIP_NORM)
    grad_gains = gain_sum * factor
    grad_conv = conv_sum * factor
    grad_qkv = qkv_part * factor
    grad_out = out_part * factor
    grad_ffn = ffn_part_grad * factor
    new_mom_qkv = MOMENTUM * mom_qkv + grad_qkv
    new_mom_out = MOMENTUM * mom_out + grad_out
    new_mom_ffn = MOMENTUM * mom_ffn + grad_ffn
    shard_rows = w_qkv.shape[1]
    head_iter = jnp.concatenate(
        [
            new_mom_qkv.reshape(3, shard_rows, heads_local, HEAD_DIM).transpose(0, 2, 1, 3),
            new_mom_out.reshape(heads_local, HEAD_DIM, shard_rows).transpose(0, 2, 1)[None],
        ],
        0,
    )
    ffn_iter = new_mom_ffn
    head_offset = head_at * heads_local
    for sweep in range(NS_ITERS):
        local_ffn = jnp.einsum("knd,kne->kde", ffn_iter, ffn_iter, precision=PRECISE)
        local_heads = jnp.einsum("kgnd,kgne->kgde", head_iter, head_iter, precision=PRECISE)
        placed = lax.dynamic_update_slice_in_dim(
            jnp.zeros((4, HEADS, HEAD_DIM, HEAD_DIM), jnp.float32), local_heads, head_offset, 1
        )
        gram_ffn, gram_placed = lax.psum((local_ffn, placed), ("head", "dp"))
        gram_heads = lax.dynamic_slice_in_dim(gram_placed, head_offset, heads_local, 1)
        if sweep == 0:
            ffn_scale = 1.0 / (jnp.sqrt(jnp.trace(gram_ffn, axis1=1, axis2=2)) + NS_EPS)
            head_scale = 1.0 / (jnp.sqrt(jnp.trace(gram_heads, axis1=2, axis2=3)) + NS_EPS)
            ffn_iter = ffn_iter * ffn_scale[:, None, None]
            gram_ffn = gram_ffn * jnp.square(ffn_scale)[:, None, None]
            head_iter = head_iter * head_scale[:, :, None, None]
            gram_heads = gram_heads * jnp.square(head_scale)[:, :, None, None]
        ffn_iter = ns_update(ffn_iter, gram_ffn)
        head_iter = ns_update(head_iter, gram_heads)
    qkv_orth = head_iter[:3].transpose(0, 2, 1, 3).reshape(3, shard_rows, cols_here)
    out_orth = head_iter[3].transpose(0, 2, 1).reshape(cols_here, shard_rows)
    new_qkv = w_qkv - RATE_IN * math.sqrt(D) * qkv_orth
    new_out = w_out - RATE_OUT * math.sqrt(D) * out_orth
    new_ffn = ffn_weights - RATE_IN * math.sqrt(max(FF, D)) * ffn_iter
    new_gain_first, new_gain_second, new_gains = adam_step(
        gains, grad_gains, gain_first, gain_second
    )
    new_conv_first, new_conv_second, new_conv = adam_step(conv, grad_conv, conv_first, conv_second)
    return (
        output,
        input_grad,
        grad_gains,
        grad_conv,
        grad_qkv,
        grad_out,
        grad_ffn,
        grad_norm,
        new_mom_qkv,
        new_mom_out,
        new_mom_ffn,
        new_gain_first,
        new_gain_second,
        new_conv_first,
        new_conv_second,
        new_gains,
        new_conv,
        new_qkv,
        new_out,
        new_ffn,
    )


def solution(mesh):
    placed = (
        P("dp", "head", None),
        P("dp"),
        P("dp", "head", None),
        P(),
        P(),
        P(None, "dp", "head"),
        P("head", "dp"),
        P(None, ("head", "dp"), None),
        P(None, "dp", "head"),
        P("head", "dp"),
        P(None, ("head", "dp"), None),
        P(),
        P(),
        P(),
        P(),
    )
    return jax.shard_map(
        per_device,
        mesh=mesh,
        in_specs=placed,
        out_specs=(
            P("dp", "head", None),
            P("dp", "head", None),
            P(),
            P(),
            P(None, "dp", "head"),
            P("head", "dp"),
            P(None, ("head", "dp"), None),
            P(),
            P(None, "dp", "head"),
            P("head", "dp"),
            P(None, ("head", "dp"), None),
            P(),
            P(),
            P(),
            P(),
            P(),
            P(),
            P(None, "dp", "head"),
            P("head", "dp"),
            P(None, ("head", "dp"), None),
        ),
        check_vma=False,
    )
```

profile of v0, /device:TPU:1, one launch (start us, length us, event | category | flops | bytes accessed | tf_op | source)
XLA Modules:
  0.0 1623.1 jit_solution(13944579310607104141)
XLA Ops:
  14.3 27.5 %all_gather.23 = bf16[192,768]{0,1:T(8,128)(2,1)S(1)} all-gather(bf16[192,24]{0,1:T(8,128)(2,1)S(1)} %convert_element_type.168), channel_id=1, replica_groups=mesh['head'=4,'dp'=32] {'dp'}, dimensions={1}, use_global_device_ids=true | all-gather | bytes 304128 | tf_op jit(solution)/shard_map/all_gather | solution.py:224
  42.8 27.0 %all_gather.22 = bf16[3,768,192]{2,1,0:T(8,128)(2,1)} all-gather(bf16[3,24,192]{2,1,0:T(8,128)(2,1)S(1)} %convert_element_type.163), channel_id=1, replica_groups=mesh['head'=4,'dp'=32] {'dp'}, dimensions={1}, use_global_device_ids=true | all-gather | bytes 912384 | tf_op jit(solution)/shard_map/all_gather | solution.py:223
  71.2 2.9 convolution_bitcast_fusion.2
  76.7 6.9 fusion.260
  83.6 6.7 fusion.261
  90.3 4.1 fusion.155
  96.8 2.7 convolution_bitcast_fusion.1
  100.2 35.9 %reduce-scatter.9.cloned.1.call-done = f32[1,256,768]{2,1,0:T(8,128)} async-done(((f32[1,1024,768]{2,1,0:T(8,128)}), f32[1,256,768]{2,1,0:T(8,128)}) %reduce-scatter.9.cloned.1.call-update) | async-done | bytes 786448 | tf_op jit(solution)/shard_map/reduce_scatter | solution.py:247
  141.5 4.2 all-gather.10.cloned.1.call-done
  145.7 27.3 %all-gather.8.cloned.1.call-done = bf16[1,1024,768]{2,1,0:T(8,128)(2,1)} async-done(((bf16[1,256,768]{2,1,0:T(8,128)(2,1)}), bf16[1,1024,768]{2,1,0:T(8,128)(2,1)}) %all-gather.8.cloned.1.call-update) | async-done | bytes 1572880 | tf_op jit(solution)/shard_map/all_gather | solution.py:252
  173.0 4.8 fusion.81
  177.8 23.7 %all-gather.12.cloned.1.call-done = bf16[1,1024,768]{2,1,0:T(8,128)(2,1)} async-done(((bf16[1,256,768]{2,1,0:T(8,128)(2,1)}), bf16[1,1024,768]{2,1,0:T(8,128)(2,1)}) %all-gather.12.cloned.1.call-update) | async-done | bytes 1572880 | tf_op jit(solution)/shard_map/all_gather | solution.py:258
  201.5 4.3 multiply_convert_fusion.2
  207.1 3.0 convolution_bitcast_fusion
  210.2 4.8 fusion.101
  215.0 33.7 %reduce-scatter.13.cloned.1.call-done = f32[1,256,768]{2,1,0:T(8,128)} async-done(((f32[1,1024,768]{2,1,0:T(8,128)}), f32[1,256,768]{2,1,0:T(8,128)}) %reduce-scatter.13.cloned.1.call-update) | async-done | bytes 786448 | tf_op jit(solution)/shard_map/reduce_scatter | solution.py:262
  248.7 2.0 multiply_reduce_fusion.5
  251.3 24.1 %reduce-scatter.11.cloned.1.call-done = bf16[1,256,768]{2,1,0:T(8,128)(2,1)} async-done(((bf16[1,1024,768]{2,1,0:T(8,128)(2,1)}), bf16[1,256,768]{2,1,0:T(8,128)(2,1)}) %reduce-scatter.11.cloned.1.call-update) | async-done | bytes 393232 | tf_op jit(solution)/shard_map/reduce_scatter | solution.py:254
  275.5 3.0 fusion.256
  278.6 3.5 fusion.108
  283.8 2.4 copy.65
  288.2 17.3 %all-gather.14.cloned.1.call-done = bf16[1,1024,768]{2,1,0:T(8,128)(2,1)} async-done(((bf16[1,256,768]{2,1,0:T(8,128)(2,1)}), bf16[1,1024,768]{2,1,0:T(8,128)(2,1)}) %all-gather.14.cloned.1.call-update) | async-done | bytes 1572880 | tf_op jit(solution)/shard_map/all_gather | solution.py:265
  305.5 2.1 fusion.132
  307.6 3.7 fusion.262
  311.3 3.6 fusion.263
  314.9 16.5 %fusion.158 = bf16[512,3,64]{0,2,1:T(8,128)(2,1)} fusion(bf16[1024,3,64]{0,2,1:T(8,128)(2,1)S(1)} %bitcast.239, f32[3,512,1024]{2,1,0:T(8,128)} %fusion.262, f32[3,512,1024]{2,1,0:T(8,128)} %get-tuple-element.216, f32[3,512]{1,0:T(4,128)} %get-tuple-element.215), kind=kOutput, calls=%fused_computation.158 | convolution fusion | flops 212437504 | bytes 13178880 | tf_op jit(solution)/shard_map/while/body/eval_jaxpr/hqk,khd->qhd/dot_general | solution.py:121
  331.5 16.4 %fusion.161 = bf16[512,3,64]{0,2,1:T(8,128)(2,1)} fusion(bf16[1024,3,64]{0,2,1:T(8,128)(2,1)S(1)} %bitcast.240, f32[3,512,1024]{2,1,0:T(8,128)} %fusion.263, f32[3,512,1024]{2,1,0:T(8,128)} %get-tuple-element.214, f32[3,512]{1,0:T(4,128)} %get-tuple-element.213), kind=kOutput, calls=%fused_computation.159 | convolution fusion | flops 212437504 | bytes 13178880 | tf_op jit(solution)/shard_map/while/body/eval_jaxpr/hqk,khd->qhd/dot_general | solution.py:121
  349.0 18.2 %fusion.40 = f32[3,64,1024]{2,1,0:T(8,128)} fusion(bf16[512,3,64]{0,2,1:T(8,128)(2,1)} %bitcast.248, f32[3,512,1024]{2,1,0:T(8,128)} %fusion.262, f32[3,512,1024]{2,1,0:T(8,128)} %get-tuple-element.216, f32[3,512]{1,0:T(4,128)} %get-tuple-element.215), kind=kOutput, calls=%fused_computation.49 | convolution fusion | flops 212339200 | bytes 13572096 | tf_op jit(solution)/shard_map/while/body/eval_jaxpr/hqk,qhd->khd/dot_general | solution.py:123
  367.1 17.3 %fusion.120 = bf16[3,64,1024]{2,1,0:T(8,128)(2,1)S(1)} fusion(f32[3,64,1024]{2,1,0:T(8,128)} %fusion.40, bf16[512,3,64]{0,2,1:T(8,128)(2,1)} %bitcast.246, f32[3,512,1024]{2,1,0:T(8,128)} %fusion.263, f32[3,512,1024]{2,1,0:T(8,128)} %get-tuple-element.214, f32[3,512]{1,0:T(4,128)} %get-tuple-element.213), kind=kOutput, calls=%fused_computation.122 | convolution fusion | flops 212732416 | bytes 13965312 | tf_op jit(solution)/shard_map/while/body/eval_jaxpr/hqk,qhd->khd/dot_general | solution.py:123
  384.4 3.6 fusion.86
  388.0 3.6 fusion.123
  395.4 2.0 fusion.111
  397.4 3.6 copy.54
  401.1 3.1 fusion.129
  404.3 4.2 fusion.100
  413.6 3.1 multiply_reduce_fusion.4
  417.0 90.4 %all-reduce.18.cloned.1.call-done = bf16[3,768,192]{2,0,1:T(4,128)(2,1)} async-done(((bf16[3,768,192]{2,0,1:T(4,128)(2,1)}), bf16[3,768,192]{2,0,1:T(4,128)(2,1)}) %all-reduce.18.cloned.1.call-update) | async-done | bytes 884752
  508.8 74.1 %reduce-scatter.17.cloned.1.call-done = bf16[192,24]{0,1:T(8,128)(2,1)} async-done(((bf16[192,768]{0,1:T(8,128)(2,1)}), bf16[192,24]{0,1:T(8,128)(2,1)}) %reduce-scatter.17.cloned.1.call-update) | async-done | bytes 9232 | tf_op jit(solution)/shard_map/reduce_scatter | solution.py:318
  586.2 25.1 %reduce-scatter.15.cloned.1.call-done = bf16[1,256,768]{2,1,0:T(8,128)(2,1)} async-done(((bf16[1,1024,768]{2,1,0:T(8,128)(2,1)}), bf16[1,256,768]{2,1,0:T(8,128)(2,1)}) %reduce-scatter.15.cloned.1.call-update) | async-done | bytes 393232 | tf_op jit(solution)/shard_map/reduce_scatter | solution.py:309
  611.3 1.9 fusion.190
  614.0 66.0 %all-reduce.5 = (f32[2,768]{1,0:T(2,128)S(1)}, f32[]{:T(128)}, f32[3,3,768]{2,1,0:T(4,128)S(1)}) all-reduce(f32[2,768]{1,0:T(2,128)S(1)} %pad_maximum_fusion.8, f32[]{:T(128)S(6)} %add.287, f32[3,3,768]{2,1,0:T(4,128)S(1)} %dynamic_update_slice.32), channel_id=1, replica_groups=mesh['head'=4,'dp'=32] {'head','dp'}, use_global_device_ids=true, to_apply=%region_16.17 | all-reduce | flops 8449 | bytes 67592 | tf_op jit(solution)/shard_map/psum | solution.py:333
  688.0 5.6 fusion.264
  696.5 154.7 %all-reduce.28.cloned.1.call-done = (f32[4,12,64,64]{3,2,1,0:T(8,128)}, f32[2,768,768]{2,1,0:T(8,128)}) async-done(((f32[4,12,64,64]{3,2,1,0:T(8,128)}, f32[2,768,768]{2,1,0:T(8,128)}), (f32[4,12,64,64]{3,2,1,0:T(8,128)}, f32[2,768,768]{2,1,0:T(8,128)})) %all-reduce.28.cloned.1.call-update) | async-done | bytes 5505040 | tf_op jit(solution)/shard_map/psum | solution.py:362
  851.2 3.3 select_reduce_fusion
  855.4 12.1 fusion.28
  867.5 3.0 fusion.164
  870.5 5.6 fusion.265
  879.1 156.8 %all-reduce.26.cloned.1.call-done = (f32[4,12,64,64]{3,2,1,0:T(8,128)}, f32[2,768,768]{2,1,0:T(8,128)}) async-done(((f32[4,12,64,64]{3,2,1,0:T(8,128)}, f32[2,768,768]{2,1,0:T(8,128)}), (f32[4,12,64,64]{3,2,1,0:T(8,128)}, f32[2,768,768]{2,1,0:T(8,128)})) %all-reduce.26.cloned.1.call-update) | async-done | bytes 5505040 | tf_op jit(solution)/shard_map/psum | solution.py:362
  1035.9 1.9 fusion.138
  1038.3 15.3 fusion.266
  1053.6 2.8 fusion.167
  1056.4 5.6 fusion.267
  1064.7 156.4 %all-reduce.24.cloned.1.call-done = (f32[4,12,64,64]{3,2,1,0:T(8,128)}, f32[2,768,768]{2,1,0:T(8,128)}) async-done(((f32[4,12,64,64]{3,2,1,0:T(8,128)}, f32[2,768,768]{2,1,0:T(8,128)}), (f32[4,12,64,64]{3,2,1,0:T(8,128)}, f32[2,768,768]{2,1,0:T(8,128)})) %all-reduce.24.cloned.1.call-update) | async-done | bytes 5505040 | tf_op jit(solution)/shard_map/psum | solution.py:362
  1221.1 1.9 fusion.137
  1223.6 15.3 fusion.268
  1238.9 2.8 fusion.170
  1241.7 5.6 fusion.269
  1249.7 156.7 %all-reduce.22.cloned.1.call-done = (f32[4,12,64,64]{3,2,1,0:T(8,128)}, f32[2,768,768]{2,1,0:T(8,128)}) async-done(((f32[4,12,64,64]{3,2,1,0:T(8,128)}, f32[2,768,768]{2,1,0:T(8,128)}), (f32[4,12,64,64]{3,2,1,0:T(8,128)}, f32[2,768,768]{2,1,0:T(8,128)})) %all-reduce.22.cloned.1.call-update) | async-done | bytes 5505040 | tf_op jit(solution)/shard_map/psum | solution.py:362
  1408.8 15.3 fusion.270
  1424.2 2.8 fusion.173
  1427.0 5.8 fusion.271
  1441.9 149.9 %all-reduce.20.cloned.1.call-done = (f32[4,12,64,64]{3,2,1,0:T(8,128)}, f32[2,768,768]{2,1,0:T(8,128)}) async-done(((f32[4,12,64,64]{3,2,1,0:T(8,128)}, f32[2,768,768]{2,1,0:T(8,128)}), (f32[4,12,64,64]{3,2,1,0:T(8,128)}, f32[2,768,768]{2,1,0:T(8,128)})) %all-reduce.20.cloned.1.call-update) | async-done | bytes 5505040 | tf_op jit(solution)/shard_map/psum | solution.py:362
  1595.8 15.3 fusion.272
  1611.1 3.5 fusion.182
  (238 shorter events, 71.8 us)
Async XLA Ops:
  8.0 63.2 %all-gather.6.cloned.1.call-start = ((), (), s32[]{:S(2)}) async-start(), calls=%async_computation.6 | async-start | bytes 1966080 | tf_op jit(solution)/shard_map/all_gather | solution.py:229
  9.2 3.5 copy-start.34
  12.0 124.1 %reduce-scatter.9.cloned.1.call-start = ((), (), s32[]{:S(2)}) async-start(), calls=%async_computation.7 | async-start | bytes 3932160 | tf_op jit(solution)/shard_map/reduce_scatter | solution.py:247
  41.8 54.9 %copy-start.7 = (bf16[192,768]{0,1:T(8,128)(2,1)}, bf16[192,768]{0,1:T(8,128)(2,1)S(1)}, u32[]{:S(2)}) copy-start(bf16[192,768]{0,1:T(8,128)(2,1)S(1)} %all_gather.23) | copy-start | bytes 884740
  42.8 31.4 %copy-start.30 = (f32[3,192]{1,0:T(4,128)}, f32[3,192]{1,0:T(4,128)S(1)}, u32[]{:S(2)}) copy-start(f32[3,192]{1,0:T(4,128)S(1)} %get-tuple-element.208) | copy-start | bytes 6916
  76.6 6.9 copy-start.22
  76.7 17.7 %copy-start.9 = (bf16[1,1,1024,192]{2,3,0,1:T(8,128)(2,1)}, bf16[1,1,1024,192]{2,3,0,1:T(8,128)(2,1)S(1)}, u32[]{:S(2)}) copy-start(bf16[1,1,1024,192]{2,3,0,1:T(8,128)(2,1)S(1)} %get-tuple-element.202) | copy-start | bytes 1179652
  90.3 4.6 copy-start.45
  90.3 4.6 copy-start.46
  94.4 1.7 copy-start.25
  96.7 2.7 copy-start.20
  96.7 39.3 %copy-start.1 = (bf16[1,256,768]{2,1,0:T(8,128)(2,1)S(1)}, bf16[1,256,768]{2,1,0:T(8,128)(2,1)}, u32[]{:S(2)}) copy-start(bf16[1,256,768]{2,1,0:T(8,128)(2,1)} %param.15) | copy-start | bytes 1179652
  99.4 46.3 %all-gather.10.cloned.1.call-start = ((), (), s32[]{:S(2)}) async-start(), calls=%async_computation.9 | async-start | bytes 2433024 | tf_op jit(solution)/shard_map/all_gather | solution.py:225
  100.2 72.8 %all-gather.8.cloned.1.call-start = ((), (), s32[]{:S(2)}) async-start(), calls=%async_computation.8 | async-start | bytes 1966080 | tf_op jit(solution)/shard_map/all_gather | solution.py:252
  138.9 62.6 %all-gather.12.cloned.1.call-start = ((), (), s32[]{:S(2)}) async-start(), calls=%async_computation.11 | async-start | bytes 1966080 | tf_op jit(solution)/shard_map/all_gather | solution.py:258
  141.5 107.3 %reduce-scatter.13.cloned.1.call-start = ((), (), s32[]{:S(2)}) async-start(), calls=%async_computation.12 | async-start | bytes 3932160 | tf_op jit(solution)/shard_map/reduce_scatter | solution.py:262
  201.5 5.6 copy-start.39
  205.8 1.3 copy-start.44
  210.1 65.3 %reduce-scatter.11.cloned.1.call-start = ((), (), s32[]{:S(2)}) async-start(), calls=%async_computation.10 | async-start | bytes 1966080 | tf_op jit(solution)/shard_map/reduce_scatter | solution.py:254
  215.0 90.5 %all-gather.14.cloned.1.call-start = ((), (), s32[]{:S(2)}) async-start(), calls=%async_computation.13 | async-start | bytes 1966080 | tf_op jit(solution)/shard_map/all_gather | solution.py:265
  278.5 131.4 %reduce-scatter.19.cloned.1.call-start = ((), (), s32[]{:S(2)}) async-start(), calls=%async_computation.16 | async-start | bytes 2433024
  278.5 3.5 copy-start.41
  278.5 3.5 copy-start.43
  286.2 19.3 %copy-start.8 = (bf16[192,768]{0,1:T(8,128)(2,1)S(1)}, bf16[192,768]{0,1:T(8,128)(2,1)}, u32[]{:S(2)}) copy-start(bf16[192,768]{0,1:T(8,128)(2,1)} %copy-done.7) | copy-start | bytes 884740
  288.1 19.5 %copy-start.10 = (bf16[1,1,1024,192]{2,3,0,1:T(8,128)(2,1)S(1)}, bf16[1,1,1024,192]{2,3,0,1:T(8,128)(2,1)}, u32[]{:S(2)}) copy-start(bf16[1,1,1024,192]{2,3,0,1:T(8,128)(2,1)} %copy-done.9) | copy-start | bytes 1179652
  288.2 219.2 %all-reduce.18.cloned.1.call-start = ((), (), s32[]{:S(2)}) async-start(), calls=%async_computation.17 | async-start | bytes 3145728
  307.6 3.7 copy-start.17
  307.6 3.7 copy-start.19
  311.3 3.6 copy-start.23
  384.4 3.6 copy-start.18
  384.4 3.6 copy-start.47
  392.4 3.0 copy-start.40
  401.1 181.9 %reduce-scatter.17.cloned.1.call-start = ((), (), s32[]{:S(2)}) async-start(), calls=%async_computation.15 | async-start | bytes 405504 | tf_op jit(solution)/shard_map/reduce_scatter | solution.py:318
  404.2 4.4 copy-start.42
  404.2 8.7 copy-start.36
  404.2 207.1 %reduce-scatter.15.cloned.1.call-start = ((), (), s32[]{:S(2)}) async-start(), calls=%async_computation.14 | async-start | bytes 1966080 | tf_op jit(solution)/shard_map/reduce_scatter | solution.py:309
  408.5 202.8 %copy-start.35 = (f32[256]{0:T(256)S(1)}, f32[256]{0:T(256)}, u32[]{:S(2)}) copy-start(f32[256]{0:T(256)} %copy-done.34) | copy-start | bytes 3076
  408.6 442.6 %all-reduce.28.cloned.1.call-start = ((), (), s32[]{:S(2)}) async-start(), calls=%async_computation.22 | async-start | bytes 12582912 | tf_op jit(solution)/shard_map/psum | solution.py:362
  679.9 4.6 copy-start.27
  679.9 6.3 copy-start.33
  684.5 1.7 copy-start.29
  688.0 179.5 %copy-start.12 = (f32[2,24,768]{2,1,0:T(8,128)}, f32[2,24,768]{2,1,0:T(8,128)S(1)}, u32[]{:S(2)}) copy-start(f32[2,24,768]{2,1,0:T(8,128)S(1)} %get-tuple-element.189) | copy-start | bytes 442372
  694.6 1.2 copy-start.3
  695.8 340.0 %all-reduce.26.cloned.1.call-start = ((), (), s32[]{:S(2)}) async-start(), calls=%async_computation.21 | async-start | bytes 12582912 | tf_op jit(solution)/shard_map/psum | solution.py:362
  851.2 3.3 copy-start.16
  851.2 4.2 copy-start
  878.9 342.3 %all-reduce.24.cloned.1.call-start = ((), (), s32[]{:S(2)}) async-start(), calls=%async_computation.20 | async-start | bytes 12582912 | tf_op jit(solution)/shard_map/psum | solution.py:362
  1037.8 15.8 slice-start.2
  1038.3 15.3 slice-start.3
  1063.1 1.2 copy-start.5
  1064.3 342.2 %all-reduce.22.cloned.1.call-start = ((), (), s32[]{:S(2)}) async-start(), calls=%async_computation.19 | async-start | bytes 12582912 | tf_op jit(solution)/shard_map/psum | solution.py:362
  1223.1 15.8 slice-start.4
  1223.6 15.3 slice-start.5
  1249.5 342.3 %all-reduce.20.cloned.1.call-start = ((), (), s32[]{:S(2)}) async-start(), calls=%async_computation.18 | async-start | bytes 12582912 | tf_op jit(solution)/shard_map/psum | solution.py:362
  1408.4 15.8 slice-start.6
  1408.8 15.3 slice-start.7
  1433.8 4.1 copy-start.32
  1433.8 6.9 copy-start.11
  1433.8 6.9 copy-start.14
  1435.0 159.4 %copy-start.28 = (f32[192,24]{0,1:T(8,128)S(1)}, f32[192,24]{0,1:T(8,128)}, u32[]{:S(2)}) copy-start(f32[192,24]{0,1:T(8,128)} %param.21) | copy-start | bytes 55300
  1435.0 160.2 %copy-start.24 = (f32[3,24,192]{2,1,0:T(8,128)S(1)}, f32[3,24,192]{2,1,0:T(8,128)}, u32[]{:S(2)}) copy-start(f32[3,24,192]{2,1,0:T(8,128)} %param.20) | copy-start | bytes 165892
  1595.2 15.9 slice-start
  1595.8 15.3 slice-start.1
  1595.8 15.3 copy-start.21
  (9 other events, 8.1 us)
Sparse Core Ops, SparseCore 0:
  12.1 29.7 all-gather.5
  99.6 36.4 reduce-scatter.8
  210.3 38.4 reduce-scatter.12
  251.0 24.4 reduce-scatter.10
  696.0 155.1 all-reduce.27
  879.0 156.8 all-reduce.25
  1064.4 156.7 all-reduce.23
  1249.6 156.7 all-reduce.21
  1435.1 156.6 all-reduce.19
Sparse Core Ops, SparseCore 1:
  102.8 42.8 all-gather.9
  147.8 25.1 all-gather.7
  175.1 26.4 all-gather.11
  278.6 26.9 all-gather.13
  309.1 78.2 reduce-scatter.18
  401.1 106.2 all-reduce.17
  510.7 72.2 reduce-scatter.16
  585.2 26.0 reduce-scatter.14
where the time goes:
time: 1630 us; the launch traced here: 1620 us
  waiting for transfers between devices  1130 us (69%)
  matrix products  272 us (17%)
  blocking collectives  120 us (7%)
  other arithmetic  46.9 us (3%)
  local copies, waits for them, and re-layouts  28.5 us (2%)
  between operations  23 us (1%)
    psum x5, waiting for transfers between devices, per_device(): gram_ffn, gram_placed = lax.psum((local_ffn, placed), ('head', 'dp'))  774 us
    unnamed x19, waiting for transfers between devices  90.7 us
    dot_general x10, matrix products, ns_update(): jnp.einsum('...de,...ef->...df', gram_matrix, gram_matrix, precision=PREC...  81.6 us
    reduce_scatter x1, waiting for transfers between devices, per_device(): lax.psum_scatter(out_grad.astype(jnp.bfloat16), 'dp', scatter_dimension=1...  74.1 us
    psum x1, blocking collectives, per_device(): lax.psum((jnp.stack([gain_one_grad, gain_two_grad]), conv_placed, squares...  66 us
    reduce_scatter x1, waiting for transfers between devices, per_device(): lax.psum_scatter(projection_portion, 'head', scatter_dimension=1, tiled=T...  35.9 us
    dot_general x2, matrix products, attend_back(): jnp.einsum('hqk,qhd->khd', score_grad, query_rows, preferred_element_type...  35.4 us
    reduce_scatter x1, waiting for transfers between devices, per_device(): lax.psum_scatter(grad_normed_part, 'head', scatter_dimension=1, tiled=True)  33.7 us
  transfers between devices with their start and end apart: 17, of which 15 were waited for; matrix products, arithmetic and copies ran while one was open for 9% of the time, Pallas kernels for 0%

commit v1 on v0

--- a/solution.py
+++ b/solution.py
@@ -173,13 +173,18 @@
     return (grad_normed, jnp.stack([input_weight_gradient, grad_back_w]))
 
 
-def ns_update(iterate, gram_matrix):
-    polynomial = COEF_B * gram_matrix + COEF_C * jnp.einsum(
-        "...de,...ef->...df", gram_matrix, gram_matrix, precision=PRECISE
-    )
-    return COEF_A * iterate + jnp.einsum(
-        "...nd,...de->...ne", iterate, polynomial, precision=PRECISE
-    )
+def ns_chain(iterate, gram_matrix):
+    identity = jnp.eye(gram_matrix.shape[-1], dtype=jnp.float32)
+
+    def times(left, right):
+        return jnp.einsum("...de,...ef->...df", left, right, precision=lax.Precision.HIGH)
+
+    for sweep in range(NS_ITERS):
+        factor = COEF_A * identity + COEF_B * gram_matrix + COEF_C * times(gram_matrix, gram_matrix)
+        iterate = times(iterate, factor)
+        if sweep < NS_ITERS - 1:
+            gram_matrix = times(times(factor, gram_matrix), factor)
+    return iterate
 
 
 def adam_step(weight, gradient, moment_one, moment_two):
@@ -353,23 +358,22 @@
     )
     ffn_iter = new_mom_ffn
     head_offset = head_at * heads_local
-    for sweep in range(NS_ITERS):
-        local_ffn = jnp.einsum("knd,kne->kde", ffn_iter, ffn_iter, precision=PRECISE)
-        local_heads = jnp.einsum("kgnd,kgne->kgde", head_iter, head_iter, precision=PRECISE)
-        placed = lax.dynamic_update_slice_in_dim(
-            jnp.zeros((4, HEADS, HEAD_DIM, HEAD_DIM), jnp.float32), local_heads, head_offset, 1
-        )
-        gram_ffn, gram_placed = lax.psum((local_ffn, placed), ("head", "dp"))
-        gram_heads = lax.dynamic_slice_in_dim(gram_placed, head_offset, heads_local, 1)
-        if sweep == 0:
-            ffn_scale = 1.0 / (jnp.sqrt(jnp.trace(gram_ffn, axis1=1, axis2=2)) + NS_EPS)
-            head_scale = 1.0 / (jnp.sqrt(jnp.trace(gram_heads, axis1=2, axis2=3)) + NS_EPS)
-            ffn_iter = ffn_iter * ffn_scale[:, None, None]
-            gram_ffn = gram_ffn * jnp.square(ffn_scale)[:, None, None]
-            head_iter = head_iter * head_scale[:, :, None, None]
-            gram_heads = gram_heads * jnp.square(head_scale)[:, :, None, None]
-        ffn_iter = ns_update(ffn_iter, gram_ffn)
-        head_iter = ns_update(head_iter, gram_heads)
+    local_ffn = jnp.einsum("knd,kne->kde", ffn_iter, ffn_iter, precision=PRECISE)
+    local_heads = jnp.einsum("kgnd,kgne->kgde", head_iter, head_iter, precision=PRECISE)
+    placed = lax.dynamic_update_slice_in_dim(
+        jnp.zeros((4, HEADS, HEAD_DIM, HEAD_DIM), jnp.float32), local_heads, head_offset, 1
+    )
+    gram_ffn, gram_placed = lax.psum((local_ffn, placed), ("head", "dp"))
+    gram_heads = lax.dynamic_slice_in_dim(gram_placed, head_offset, heads_local, 1)
+    ffn_scale = 1.0 / (jnp.sqrt(jnp.trace(gram_ffn, axis1=1, axis2=2)) + NS_EPS)
+    head_scale = 1.0 / (jnp.sqrt(jnp.trace(gram_heads, axis1=2, axis2=3)) + NS_EPS)
+    ffn_iter = ns_chain(
+        ffn_iter * ffn_scale[:, None, None], gram_ffn * jnp.square(ffn_scale)[:, None, None]
+    )
+    head_iter = ns_chain(
+        head_iter * head_scale[:, :, None, None],
+        gram_heads * jnp.square(head_scale)[:, :, None, None],
+    )
     qkv_orth = head_iter[:3].transpose(0, 2, 1, 3).reshape(3, shard_rows, cols_here)
     out_orth = head_iter[3].transpose(0, 2, 1).reshape(cols_here, shard_rows)
     new_qkv = w_qkv - RATE_IN * math.sqrt(D) * qkv_orth

time: 1630 us -> 955 us (0.59)
  waiting for transfers between devices: 1130 us -> 513 us
  matrix products: 272 us -> 228 us
    psum x5 -> x1, waiting for transfers between devices: 774 us -> 145 us  [per_device(): gram_ffn, gram_placed = lax.psum((local_ffn, placed), ('head', 'dp'))]
    dot_general x5 -> x1, matrix products: 28.2 us -> 5.57 us  [per_device(): jnp.einsum('knd,kne->kde', ffn_iter, ffn_iter, precision=PRECISE)]
    unnamed x19 -> x15, waiting for transfers between devices: 90.7 us -> 102 us
    dot_general x20 -> x36, matrix products: 98.8 us -> 103 us  [times(): jnp.einsum('...de,...ef->...df', left, right, precision=lax.Precision.HIGH)]
  transfers between devices with their start and end apart: 17 -> 13, of which waited for: 15 -> 11; matrix products, arithmetic and copies ran while one was open for 9% -> 14% of each run, Pallas kernels for 0% -> 0%
where the time goes in v1:
time: 955 us; the launch traced here: 951 us
  waiting for transfers between devices  513 us (54%)
  matrix products  228 us (24%)
  blocking collectives  119 us (12%)
  other arithmetic  44.4 us (5%)
  between operations  23 us (2%)
  local copies, waits for them, and re-layouts  22.8 us (2%)
    psum x1, waiting for transfers between devices, per_device(): gram_ffn, gram_placed = lax.psum((local_ffn, placed), ('head', 'dp'))  145 us
    dot_general x36, matrix products, times(): jnp.einsum('...de,...ef->...df', left, right, precision=lax.Precision.HIGH)  103 us
    unnamed x15, waiting for transfers between devices  102 us
    reduce_scatter x1, waiting for transfers between devices, per_device(): lax.psum_scatter(out_grad.astype(jnp.bfloat16), 'dp', scatter_dimension=1...  74.1 us
    psum x1, blocking collectives, per_device(): lax.psum((jnp.stack([gain_one_grad, gain_two_grad]), conv_placed, squares...  66.4 us
    reduce_scatter x1, waiting for transfers between devices, per_device(): lax.psum_scatter(projection_portion, 'head', scatter_dimension=1, tiled=T...  35.9 us
    reduce_scatter x1, waiting for transfers between devices, per_device(): lax.psum_scatter(grad_normed_part, 'head', scatter_dimension=1, tiled=True)  33.7 us
    all_gather x1, blocking collectives, per_device(): lax.all_gather(w_out.astype(jnp.bfloat16), 'dp', axis=1, tiled=True)  27.5 us
  transfers between devices with their start and end apart: 13, of which 11 were waited for; matrix products, arithmetic and copies ran while one was open for 14% of the time, Pallas kernels for 0%

profile of v1, /device:TPU:1, one launch (start us, length us, event | category | flops | bytes accessed | tf_op | source)
XLA Modules:
  0.0 950.7 jit_solution(1951191519190957339)
XLA Ops:
  10.0 1.9 fusion.215
  14.3 27.5 %all_gather.23 = bf16[192,768]{0,1:T(8,128)(2,1)S(1)} all-gather(bf16[192,24]{0,1:T(8,128)(2,1)S(1)} %convert_element_type.170), channel_id=1, replica_groups=mesh['head'=4,'dp'=32] {'dp'}, dimensions={1}, use_global_device_ids=true | all-gather | bytes 304128 | tf_op jit(solution)/shard_map/all_gather | solution.py:229
  42.6 24.8 %all_gather.22 = bf16[3,768,192]{2,1,0:T(8,128)(2,1)S(1)} all-gather(bf16[3,24,192]{2,1,0:T(8,128)(2,1)S(1)} %convert_element_type.165), channel_id=1, replica_groups=mesh['head'=4,'dp'=32] {'dp'}, dimensions={1}, use_global_device_ids=true | all-gather | bytes 912384 | tf_op jit(solution)/shard_map/all_gather | solution.py:228
  68.1 2.5 convolution_bitcast_fusion.2
  73.9 5.0 fusion.301
  78.9 5.0 fusion.302
  83.9 4.1 fusion.197
  89.7 2.3 convolution_bitcast_fusion.1
  93.3 35.9 %reduce-scatter.9.cloned.1.call-done = f32[1,256,768]{2,1,0:T(8,128)} async-done(((f32[1,1024,768]{2,1,0:T(8,128)}), f32[1,256,768]{2,1,0:T(8,128)}) %reduce-scatter.9.cloned.1.call-update) | async-done | bytes 786448 | tf_op jit(solution)/shard_map/reduce_scatter | solution.py:252
  132.5 6.4 all-gather.10.cloned.1.call-done
  138.9 27.3 %all-gather.8.cloned.1.call-done = bf16[1,1024,768]{2,1,0:T(8,128)(2,1)} async-done(((bf16[1,256,768]{2,1,0:T(8,128)(2,1)}), bf16[1,1024,768]{2,1,0:T(8,128)(2,1)}) %all-gather.8.cloned.1.call-update) | async-done | bytes 1572880 | tf_op jit(solution)/shard_map/all_gather | solution.py:257
  166.2 4.8 fusion.123
  171.0 23.7 %all-gather.12.cloned.1.call-done = bf16[1,1024,768]{2,1,0:T(8,128)(2,1)} async-done(((bf16[1,256,768]{2,1,0:T(8,128)(2,1)}), bf16[1,1024,768]{2,1,0:T(8,128)(2,1)}) %all-gather.12.cloned.1.call-update) | async-done | bytes 1572880 | tf_op jit(solution)/shard_map/all_gather | solution.py:263
  194.7 4.3 multiply_convert_fusion.2
  200.2 3.0 convolution_bitcast_fusion
  203.3 4.8 fusion.143
  208.2 33.7 %reduce-scatter.13.cloned.1.call-done = f32[1,256,768]{2,1,0:T(8,128)} async-done(((f32[1,1024,768]{2,1,0:T(8,128)}), f32[1,256,768]{2,1,0:T(8,128)}) %reduce-scatter.13.cloned.1.call-update) | async-done | bytes 786448 | tf_op jit(solution)/shard_map/reduce_scatter | solution.py:267
  241.8 2.0 multiply_reduce_fusion.5
  243.9 24.6 %reduce-scatter.11.cloned.1.call-done = bf16[1,256,768]{2,1,0:T(8,128)(2,1)} async-done(((bf16[1,1024,768]{2,1,0:T(8,128)(2,1)}), bf16[1,256,768]{2,1,0:T(8,128)(2,1)}) %reduce-scatter.11.cloned.1.call-update) | async-done | bytes 393232 | tf_op jit(solution)/shard_map/reduce_scatter | solution.py:259
  268.5 2.8 fusion.297
  271.4 3.5 fusion.150
  274.9 2.9 fusion.147
  278.0 2.4 copy.65
  280.4 1.9 copy.67
  282.6 15.8 %all-gather.14.cloned.1.call-done = bf16[1,1024,768]{2,1,0:T(8,128)(2,1)} async-done(((bf16[1,256,768]{2,1,0:T(8,128)(2,1)}), bf16[1,1024,768]{2,1,0:T(8,128)(2,1)}) %all-gather.14.cloned.1.call-update) | async-done | bytes 1572880 | tf_op jit(solution)/shard_map/all_gather | solution.py:270
  298.4 2.1 fusion.174
  300.5 3.6 fusion.303
  304.1 3.6 fusion.304
  307.7 12.4 %fusion.200 = bf16[512,3,64]{0,2,1:T(8,128)(2,1)S(1)} fusion(bf16[1024,3,64]{0,2,1:T(8,128)(2,1)S(1)} %bitcast.247, f32[3,512,1024]{2,1,0:T(8,128)} %fusion.303, f32[3,512,1024]{2,1,0:T(8,128)} %get-tuple-element.208, f32[3,512]{1,0:T(4,128)S(1)} %get-tuple-element.207), kind=kOutput, calls=%fused_computation.201 | convolution fusion | flops 212437504 | bytes 13178880 | tf_op jit(solution)/shard_map/while/body/eval_jaxpr/hqk,khd->qhd/dot_general | solution.py:121
  320.2 12.6 %fusion.203 = bf16[512,3,64]{0,2,1:T(8,128)(2,1)S(1)} fusion(bf16[1024,3,64]{0,2,1:T(8,128)(2,1)S(1)} %bitcast.248, f32[3,512,1024]{2,1,0:T(8,128)} %fusion.304, f32[3,512,1024]{2,1,0:T(8,128)} %get-tuple-element.206, f32[3,512]{1,0:T(4,128)S(1)} %get-tuple-element.205), kind=kOutput, calls=%fused_computation.202 | convolution fusion | flops 212437504 | bytes 13178880 | tf_op jit(solution)/shard_map/while/body/eval_jaxpr/hqk,khd->qhd/dot_general | solution.py:121
  332.9 13.3 %fusion.51 = f32[3,64,1024]{2,1,0:T(8,128)S(1)} fusion(bf16[512,3,64]{0,2,1:T(8,128)(2,1)S(1)} %bitcast.258, f32[3,512,1024]{2,1,0:T(8,128)} %fusion.303, f32[3,512,1024]{2,1,0:T(8,128)} %get-tuple-element.208, f32[3,512]{1,0:T(4,128)S(1)} %get-tuple-element.207), kind=kOutput, calls=%fused_computation.64 | convolution fusion | flops 212339200 | bytes 13572096 | tf_op jit(solution)/shard_map/while/body/eval_jaxpr/hqk,qhd->khd/dot_general | solution.py:123
  346.2 13.3 %fusion.162 = bf16[3,64,1024]{2,1,0:T(8,128)(2,1)S(1)} fusion(f32[3,64,1024]{2,1,0:T(8,128)S(1)} %fusion.51, bf16[512,3,64]{0,2,1:T(8,128)(2,1)S(1)} %bitcast.256, f32[3,512,1024]{2,1,0:T(8,128)} %fusion.304, f32[3,512,1024]{2,1,0:T(8,128)} %get-tuple-element.206, f32[3,512]{1,0:T(4,128)S(1)} %copy-done.38), kind=kOutput, calls=%fused_computation.168 | convolution fusion | flops 212732416 | bytes 13965312 | tf_op jit(solution)/shard_map/while/body/eval_jaxpr/hqk,qhd->khd/dot_general | solution.py:123
  359.5 3.6 fusion.128
  363.1 3.5 fusion.165
  370.2 2.0 fusion.153
  372.2 3.5 copy.54
  377.4 4.4 fusion.142
  386.8 3.0 multiply_reduce_fusion.4
  390.2 100.7 %all-reduce.10.cloned.1.call-done = bf16[3,768,192]{2,0,1:T(4,128)(2,1)} async-done(((bf16[3,768,192]{2,0,1:T(4,128)(2,1)}), bf16[3,768,192]{2,0,1:T(4,128)(2,1)}) %all-reduce.10.cloned.1.call-update) | async-done | bytes 884752
  492.4 74.1 %reduce-scatter.17.cloned.1.call-done = bf16[192,24]{0,1:T(8,128)(2,1)} async-done(((bf16[192,768]{0,1:T(8,128)(2,1)}), bf16[192,24]{0,1:T(8,128)(2,1)}) %reduce-scatter.17.cloned.1.call-update) | async-done | bytes 9232 | tf_op jit(solution)/shard_map/reduce_scatter | solution.py:323
  569.8 25.1 %reduce-scatter.15.cloned.1.call-done = bf16[1,256,768]{2,1,0:T(8,128)(2,1)} async-done(((bf16[1,1024,768]{2,1,0:T(8,128)(2,1)}), bf16[1,256,768]{2,1,0:T(8,128)(2,1)}) %reduce-scatter.15.cloned.1.call-update) | async-done | bytes 393232 | tf_op jit(solution)/shard_map/reduce_scatter | solution.py:314
  594.9 1.9 fusion.217
  597.5 66.4 %all-reduce.5 = (f32[2,768]{1,0:T(2,128)S(1)}, f32[]{:T(128)}, f32[3,3,768]{2,1,0:T(4,128)S(1)}) all-reduce(f32[2,768]{1,0:T(2,128)S(1)} %pad_maximum_fusion.8, f32[]{:T(128)S(6)} %add.313, f32[3,3,768]{2,1,0:T(4,128)S(1)} %dynamic_update_slice.20), channel_id=1, replica_groups=mesh['head'=4,'dp'=32] {'head','dp'}, use_global_device_ids=true, to_apply=%region_16.17 | all-reduce | flops 8449 | bytes 67592 | tf_op jit(solution)/shard_map/psum | solution.py:338
  672.6 5.6 fusion.316
  688.9 2.1 fusion.214
  691.0 144.6 %all-reduce.12.cloned.1.call-done = (f32[4,12,64,64]{3,2,1,0:T(8,128)}, f32[2,768,768]{2,1,0:T(8,128)}) async-done(((f32[4,12,64,64]{3,2,1,0:T(8,128)}, f32[2,768,768]{2,1,0:T(8,128)}), (f32[4,12,64,64]{3,2,1,0:T(8,128)}, f32[2,768,768]{2,1,0:T(8,128)})) %all-reduce.12.cloned.1.call-update) | async-done | bytes 5505040 | tf_op jit(solution)/shard_map/psum | solution.py:366
  849.4 10.2 %fusion.43 = f32[2,768,768]{2,1,0:T(8,128)S(1)} fusion(f32[2,768,768]{2,1,0:T(8,128)} %get-tuple-element.170, f32[2]{0:T(128)S(1)} %get-tuple-element.171), kind=kOutput, calls=%fused_computation.52 | convolution fusion | flops 5436997632 | bytes 9437192 | tf_op jit(solution)/shard_map/...de,...ef->...df/dot_general | solution.py:180
  859.6 6.1 fusion.32
  865.7 1.9 fusion.33
  867.6 6.4 fusion.31
  874.1 5.8 fusion.317
  879.9 6.4 fusion.26
  886.3 1.8 fusion.27
  888.1 5.9 fusion.25
  894.0 6.0 fusion.318
  900.0 5.9 fusion.20
  905.9 1.8 fusion.21
  907.7 6.1 fusion.19
  913.9 5.8 fusion.319
  919.7 6.3 fusion.14
  926.1 1.8 fusion.15
  927.9 5.9 fusion.13
  933.8 6.0 fusion.320
  939.8 2.5 fusion.209
  (204 shorter events, 60.7 us)
Async XLA Ops:
  8.0 60.0 %all-gather.6.cloned.1.call-start = ((), (), s32[]{:S(2)}) async-start(), calls=%async_computation.6 | async-start | bytes 1966080 | tf_op jit(solution)/shard_map/all_gather | solution.py:234
  9.2 2.8 copy-start.28
  12.0 117.3 %reduce-scatter.9.cloned.1.call-start = ((), (), s32[]{:S(2)}) async-start(), calls=%async_computation.7 | async-start | bytes 3932160 | tf_op jit(solution)/shard_map/reduce_scatter | solution.py:252
  67.5 6.3 copy-start.12
  70.6 1.5 copy-start.1
  73.9 5.0 copy-start.20
  73.9 5.0 copy-start.22
  78.9 241.3 %copy-start.37 = (f32[3,512]{1,0:T(4,128)}, f32[3,512]{1,0:T(4,128)S(1)}, u32[]{:S(2)}) copy-start(f32[3,512]{1,0:T(4,128)S(1)} %get-tuple-element.205) | copy-start | bytes 18436
  83.8 4.6 copy-start.36
  89.6 3.0 copy-start.16
  89.6 39.6 %copy-start = (bf16[1,256,768]{2,1,0:T(8,128)(2,1)S(1)}, bf16[1,256,768]{2,1,0:T(8,128)(2,1)}, u32[]{:S(2)}) copy-start(bf16[1,256,768]{2,1,0:T(8,128)(2,1)} %param.15) | copy-start | bytes 1179652
  89.7 41.9 %copy-start.9 = (bf16[1,256,768]{2,1,0:T(8,128)(2,1)S(1)}, bf16[1,256,768]{2,1,0:T(8,128)(2,1)}, u32[]{:S(2)}) copy-start(bf16[1,256,768]{2,1,0:T(8,128)(2,1)} %param.17) | copy-start | bytes 1179652
  92.6 46.3 %all-gather.10.cloned.1.call-start = ((), (), s32[]{:S(2)}) async-start(), calls=%async_computation.9 | async-start | bytes 2433024 | tf_op jit(solution)/shard_map/all_gather | solution.py:230
  93.3 72.9 %all-gather.8.cloned.1.call-start = ((), (), s32[]{:S(2)}) async-start(), calls=%async_computation.8 | async-start | bytes 1966080 | tf_op jit(solution)/shard_map/all_gather | solution.py:257
  131.5 63.2 %all-gather.12.cloned.1.call-start = ((), (), s32[]{:S(2)}) async-start(), calls=%async_computation.11 | async-start | bytes 1966080 | tf_op jit(solution)/shard_map/all_gather | solution.py:263
  132.5 109.3 %reduce-scatter.13.cloned.1.call-start = ((), (), s32[]{:S(2)}) async-start(), calls=%async_computation.12 | async-start | bytes 3932160 | tf_op jit(solution)/shard_map/reduce_scatter | solution.py:267
  194.7 5.5 copy-start.31
  199.0 1.2 copy-start.35
  203.2 65.2 %reduce-scatter.11.cloned.1.call-start = ((), (), s32[]{:S(2)}) async-start(), calls=%async_computation.10 | async-start | bytes 1966080 | tf_op jit(solution)/shard_map/reduce_scatter | solution.py:259
  208.1 90.3 %all-gather.14.cloned.1.call-start = ((), (), s32[]{:S(2)}) async-start(), calls=%async_computation.13 | async-start | bytes 1966080 | tf_op jit(solution)/shard_map/all_gather | solution.py:270
  271.3 111.8 %reduce-scatter.19.cloned.1.call-start = ((), (), s32[]{:S(2)}) async-start(), calls=%async_computation.16 | async-start | bytes 2433024
  271.4 3.5 copy-start.34
  282.4 208.6 %all-reduce.10.cloned.1.call-start = ((), (), s32[]{:S(2)}) async-start(), calls=%async_computation.17 | async-start | bytes 3145728
  320.2 12.7 %copy-start.23 = (bf16[1,1,512,192]{2,3,0,1:T(8,128)(2,1)S(1)}, bf16[1,1,512,192]{2,3,0,1:T(8,128)(2,1)}, u32[]{:S(2)}) copy-start(bf16[1,1,512,192]{2,3,0,1:T(8,128)(2,1)} %copy-done.22) | copy-start | bytes 589828
  332.9 13.3 %copy-start.21 = (bf16[1,1,512,192]{2,3,0,1:T(8,128)(2,1)S(1)}, bf16[1,1,512,192]{2,3,0,1:T(8,128)(2,1)}, u32[]{:S(2)}) copy-start(bf16[1,1,512,192]{2,3,0,1:T(8,128)(2,1)} %copy-done.20) | copy-start | bytes 589828
  332.9 13.3 %copy-start.38 = (f32[3,512]{1,0:T(4,128)S(1)}, f32[3,512]{1,0:T(4,128)}, u32[]{:S(2)}) copy-start(f32[3,512]{1,0:T(4,128)} %copy-done.37) | copy-start | bytes 18436
  366.7 0.8 copy-start.10
  366.7 3.6 copy-start.32
  369.2 1.0 copy-start.13
  370.2 5.5 copy-start.8
  375.7 190.8 %reduce-scatter.17.cloned.1.call-start = ((), (), s32[]{:S(2)}) async-start(), calls=%async_computation.15 | async-start | bytes 405504 | tf_op jit(solution)/shard_map/reduce_scatter | solution.py:323
  377.3 4.6 copy-start.33
  377.3 8.9 copy-start.30
  377.3 9.5 copy-start.2
  377.3 217.6 %reduce-scatter.15.cloned.1.call-start = ((), (), s32[]{:S(2)}) async-start(), calls=%async_computation.14 | async-start | bytes 1966080 | tf_op jit(solution)/shard_map/reduce_scatter | solution.py:314
  381.8 213.1 %copy-start.29 = (f32[256]{0:T(256)S(1)}, f32[256]{0:T(256)}, u32[]{:S(2)}) copy-start(f32[256]{0:T(256)} %copy-done.28) | copy-start | bytes 3076
  381.8 453.8 %all-reduce.12.cloned.1.call-start = ((), (), s32[]{:S(2)}) async-start(), calls=%async_computation.18 | async-start | bytes 12582912 | tf_op jit(solution)/shard_map/psum | solution.py:366
  663.9 4.6 copy-start.24
  663.9 4.7 copy-start.27
  668.5 0.6 copy-start.26
  669.1 11.2 %copy-start.18 = (f32[3,64,24]{1,2,0:T(8,128)}, f32[3,64,24]{1,2,0:T(8,128)S(1)}, u32[]{:S(2)}) copy-start(f32[3,64,24]{1,2,0:T(8,128)S(1)} %copy.77) | copy-start | bytes 55300
  670.8 7.4 copy-start.15
  670.9 7.5 copy-start.14
  672.6 5.6 copy-start.6
  679.2 1.1 copy-start.3
  679.2 9.7 %copy-start.4 = (f32[1,256,768]{2,1,0:T(8,128)S(1)}, f32[1,256,768]{2,1,0:T(8,128)}, u32[]{:S(2)}) copy-start(f32[1,256,768]{2,1,0:T(8,128)} %get-tuple-element.186) | copy-start | bytes 2359300
  691.0 152.7 %copy-start.11 = (f32[64,64]{1,0:T(8,128)S(1)}, f32[64,64]{1,0:T(8,128)}, u32[]{:S(2)}) copy-start(f32[64,64]{1,0:T(8,128)} %broadcast_select_fusion.1) | copy-start | bytes 49156
  841.5 5.5 slice-start
  844.1 3.0 copy-start.5
  844.4 2.7 slice-start.1
  845.7 2.3 copy-start.25
  846.0 2.8 copy-start.19
  849.4 10.2 %slice-start.2 = ((s8[4718592]{0:T(1024)(128)(4,1)}), s8[4194304]{0:T(1024)(128)(4,1)S(1)}, s32[]{:S(2)}) async-start(s8[4718592]{0:T(1024)(128)(4,1)} %bitcast.222), calls=%async_computation.21 | async-start | bytes 8388608
  849.4 10.2 %slice-start.3 = ((s8[4718592]{0:T(1024)(128)(4,1)}), s8[524288]{0:T(1024)(128)(4,1)S(1)}, s32[]{:S(2)}) async-start(s8[4718592]{0:T(1024)(128)(4,1)} %bitcast.222), calls=%async_computation.22 | async-start | bytes 1048576
  859.6 6.1 copy-start.7
  933.8 6.0 copy-start.17
Sparse Core Ops, SparseCore 0:
  12.1 29.7 all-gather.5
  92.7 36.4 reduce-scatter.8
  203.4 38.4 reduce-scatter.12
  244.1 24.3 reduce-scatter.10
  680.5 155.1 all-reduce.11
Sparse Core Ops, SparseCore 1:
  96.0 42.9 all-gather.9
  141.0 25.1 all-gather.7
  168.3 26.4 all-gather.11
  271.4 27.0 all-gather.13
  302.0 78.0 reduce-scatter.18
  383.7 107.1 all-reduce.9
  494.3 72.2 reduce-scatter.16
  568.8 26.0 reduce-scatter.14

commit v2 on v0

--- a/solution.py
+++ b/solution.py
@@ -3,6 +3,8 @@
 import jax
 import jax.numpy as jnp
 from jax import lax
+from jax.experimental import pallas as pl
+from jax.experimental.pallas import tpu as pltpu
 from jax.sharding import PartitionSpec as P
 
 D = 768
@@ -173,13 +175,388 @@
     return (grad_normed, jnp.stack([input_weight_gradient, grad_back_w]))
 
 
-def ns_update(iterate, gram_matrix):
-    polynomial = COEF_B * gram_matrix + COEF_C * jnp.einsum(
-        "...de,...ef->...df", gram_matrix, gram_matrix, precision=PRECISE
-    )
-    return COEF_A * iterate + jnp.einsum(
-        "...nd,...de->...ne", iterate, polynomial, precision=PRECISE
-    )
+SUB = 24
+PAIR = 2 * SUB
+BLK = 256
+MESH_IDS = pl.DeviceIdType.MESH
+
+
+def place():
+    flat = lax.axis_index("dp")
+    return flat // 8, lax.axis_index("head"), (flat // 2) % 4, flat % 2
+
+
+def device(x, y, z, core):
+    return (y % 4, ((x % 4) * 4 + z % 4) * 2 + core)
+
+
+def greet(others):
+    barrier = pltpu.get_barrier_semaphore()
+    for other in others:
+        pl.semaphore_signal(barrier, inc=1, device_id=other, device_id_type=MESH_IDS)
+    pl.semaphore_wait(barrier, len(others))
+
+
+def send(source, target, sems, index, other):
+    copy = pltpu.make_async_remote_copy(
+        src_ref=source,
+        dst_ref=target,
+        send_sem=sems[0].at[index],
+        recv_sem=sems[1].at[index],
+        device_id=other,
+        device_id_type=MESH_IDS,
+    )
+    copy.start()
+    return copy
+
+
+def rows(start, count):
+    return pl.ds(pl.multiple_of(start, 8), count)
+
+
+def split(values):
+    high = values.astype(jnp.bfloat16)
+    return high, (values - high.astype(jnp.float32)).astype(jnp.bfloat16)
+
+
+def product(left, right, dims=(((1,), (0,)), ((), ()))):
+    lh, ll = left
+    rh, rl = right
+
+    def dot(a, b):
+        return lax.dot_general(a, b, dims, preferred_element_type=jnp.float32)
+
+    return dot(lh, rh) + (dot(lh, rl) + dot(ll, rh))
+
+
+UPPER = ((0, 0), (0, 1), (0, 2), (1, 1), (1, 2), (2, 2))
+
+
+def sum_kernel(
+    g_ffn, g_heads, m_ffn, m_heads, small,
+    small_out, gram_out, hgram_out, x_out, xh_out,
+    gin, min_, ghin, mhin, s_core, s_x, s_z, s_y, part, r_one, r_two, r_three, hpart, hr_one, hr_two,
+    send_sem, recv_sem,
+):
+    x, y, z, core = place()
+    sems = (send_sem, recv_sem)
+    sibling = device(x, y, z, 1 - core)
+    along = {
+        "x": [device(x + k, y, z, core) for k in (1, 2, 3)],
+        "z": [device(x, y, z + k, core) for k in (1, 2, 3)],
+        "y": [device(x, y + k, z, core) for k in (1, 2, 3)],
+    }
+    greet([sibling] + along["x"] + along["z"] + along["y"])
+    swaps = [
+        send(g_ffn.at[1 - core], gin, sems, 0, sibling),
+        send(m_ffn.at[1 - core], min_, sems, 1, sibling),
+        send(g_heads.at[pl.ds(2 - 2 * core, 2)], ghin, sems, 2, sibling),
+        send(m_heads.at[pl.ds(2 - 2 * core, 2)], mhin, sems, 3, sibling),
+    ]
+    lanes_ffn = jnp.sum(g_ffn[...] * g_ffn[...], axis=(0, 1))
+    lanes_heads = jnp.sum(g_heads[...] * g_heads[...], axis=(0, 1))
+    own = small[...]
+    row_ids = lax.broadcasted_iota(jnp.int32, own.shape, 0)
+    wide = jnp.concatenate([lanes_heads, jnp.zeros((D - lanes_heads.shape[0],), jnp.float32)])
+    own = own + jnp.where(row_ids == 11, lanes_ffn[None, :] + wide[None, :], 0.0)
+    number = 4
+    s_core[core] = own
+    copy = send(s_core.at[core], s_core.at[core], sems, number, sibling)
+    copy.wait()
+    total = s_core[0] + s_core[1]
+    number = 5
+    for slots, axis, here in ((s_x, "x", x), (s_z, "z", z), (s_y, "y", y)):
+        slots[here] = total
+        copies = [
+            send(slots.at[here], slots.at[here], sems, number + k, along[axis][k]) for k in range(3)
+        ]
+        for copy in copies:
+            copy.wait()
+        total = (slots[0] + slots[1]) + (slots[2] + slots[3])
+        number += 3
+    small_out[...] = total
+    squared = jnp.sum(jnp.where(row_ids < 11, total * total, total), axis=(0, 1), keepdims=True)
+    factor = CLIP_NORM / jnp.maximum(jnp.sqrt(squared), CLIP_NORM)
+    for copy in swaps:
+        copy.wait()
+    here_rows = MOMENTUM * m_ffn[core] + factor * g_ffn[core]
+    there_rows = MOMENTUM * min_[...] + factor * gin[...]
+    x_out[rows(core * SUB, SUB), :] = here_rows
+    x_out[rows((1 - core) * SUB, SUB), :] = there_rows
+    for kind in range(2):
+        xh_out[kind, rows(core * SUB, SUB), :] = (
+            MOMENTUM * m_heads[2 * core + kind] + factor * g_heads[2 * core + kind]
+        )
+        xh_out[kind, rows((1 - core) * SUB, SUB), :] = MOMENTUM * mhin[kind] + factor * ghin[kind]
+    transposed = (((0,), (0,)), ((), ()))
+    for number_of, (i, j) in enumerate(UPPER):
+        part[number_of * BLK : (number_of + 1) * BLK, :] = product(
+            split(x_out[:, i * BLK : (i + 1) * BLK]),
+            split(x_out[:, j * BLK : (j + 1) * BLK]),
+            transposed,
+        )
+    columns = xh_out.shape[2]
+    r_ids = lax.broadcasted_iota(jnp.int32, (columns, columns), 0) // HEAD_DIM
+    c_ids = lax.broadcasted_iota(jnp.int32, (columns, columns), 1) // HEAD_DIM
+    packed = []
+    for kind in range(2):
+        pieces = split(xh_out[kind])
+        gram = jnp.where(r_ids == c_ids, product(pieces, pieces, transposed), 0.0)
+        folded = gram[:, :HEAD_DIM]
+        for head in range(1, columns // HEAD_DIM):
+            folded = folded + gram[:, head * HEAD_DIM : (head + 1) * HEAD_DIM]
+        packed.append(folded)
+    hpart[columns:, :] = jnp.zeros((hpart.shape[0] - columns, 2 * HEAD_DIM), jnp.float32)
+    hpart[:columns, :] = jnp.concatenate(packed, axis=1)
+    one = x + core * (z - x)
+    two = z + core * (x - z)
+    first = [device(x + k * (1 - core), y, z + k * core, core) for k in (1, 2, 3)]
+    second = [device(x + k * core, y, z + k * (1 - core), core) for k in (1, 2, 3)]
+    n_one, n_two, n_three = part.shape[0] // 4, part.shape[0] // 16, part.shape[0] // 64
+    h_one, h_two = hpart.shape[0] // 4, hpart.shape[0] // 16
+
+    copies = []
+    for k in range(3):
+        to = (one + k + 1) % 4
+        copies.append(send(part.at[rows(to * n_one, n_one)], r_one.at[k], sems, 14 + k, first[k]))
+        copies.append(send(hpart.at[rows(to * h_one, h_one)], hr_one.at[k], sems, 17 + k, first[k]))
+    for copy in copies:
+        copy.wait()
+    base = one * n_one
+    hbase = one * h_one
+    part[rows(base, n_one), :] += (r_one[0] + r_one[1]) + r_one[2]
+    hpart[rows(hbase, h_one), :] += (hr_one[0] + hr_one[1]) + hr_one[2]
+    copies = []
+    for k in range(3):
+        to = (two + k + 1) % 4
+        copies.append(
+            send(part.at[rows(base + to * n_two, n_two)], r_two.at[k], sems, 20 + k, second[k])
+        )
+        copies.append(
+            send(hpart.at[rows(hbase + to * h_two, h_two)], hr_two.at[k], sems, 23 + k, second[k])
+        )
+    for copy in copies:
+        copy.wait()
+    base2 = base + two * n_two
+    hbase2 = hbase + two * h_two
+    part[rows(base2, n_two), :] += (r_two[0] + r_two[1]) + r_two[2]
+    hgram_out[rows(hbase2, h_two), :] = (
+        hpart[rows(hbase2, h_two), :] + (hr_two[0] + hr_two[1]) + hr_two[2]
+    )
+    copies = []
+    for k in range(3):
+        to = (y + k + 1) % 4
+        copies.append(
+            send(part.at[rows(base2 + to * n_three, n_three)], r_three.at[k], sems, 26 + k, along["y"][k])
+        )
+    for copy in copies:
+        copy.wait()
+    base3 = base2 + y * n_three
+    gram_out[rows(base3, n_three), :] = (
+        part[rows(base3, n_three), :] + (r_three[0] + r_three[1]) + r_three[2]
+    )
+    number = 29
+    for others, start, count, hstart, hcount in (
+        (along["y"], base3, n_three, None, None),
+        (second, base2, n_two, hbase2, h_two),
+        (first, base, n_one, hbase, h_one),
+    ):
+        copies = []
+        for k in range(3):
+            region = gram_out.at[rows(start, count)]
+            copies.append(send(region, region, sems, number + k, others[k]))
+            if hstart is not None:
+                region = hgram_out.at[rows(hstart, hcount)]
+                copies.append(send(region, region, sems, number + 3 + k, others[k]))
+        for copy in copies:
+            copy.wait()
+        number += 3 if hstart is None else 6
+
+
+def sum_over_devices(g_ffn, g_heads, m_ffn, m_heads, small):
+    f32 = jnp.float32
+    cols = g_heads.shape[2]
+    vmem = pl.BlockSpec(memory_space=pltpu.VMEM)
+    return pl.pallas_call(
+        sum_kernel,
+        out_shape=[
+            jax.ShapeDtypeStruct((16, D), f32),
+            jax.ShapeDtypeStruct((6 * BLK, BLK), f32),
+            jax.ShapeDtypeStruct((BLK, 2 * HEAD_DIM), f32),
+            jax.ShapeDtypeStruct((PAIR, D), f32),
+            jax.ShapeDtypeStruct((2, PAIR, cols), f32),
+        ],
+        in_specs=[vmem] * 5,
+        out_specs=[vmem] * 5,
+        scratch_shapes=[
+            pltpu.VMEM((SUB, D), f32),
+            pltpu.VMEM((SUB, D), f32),
+            pltpu.VMEM((2, SUB, cols), f32),
+            pltpu.VMEM((2, SUB, cols), f32),
+            pltpu.VMEM((2, 16, D), f32),
+            pltpu.VMEM((4, 16, D), f32),
+            pltpu.VMEM((4, 16, D), f32),
+            pltpu.VMEM((4, 16, D), f32),
+            pltpu.VMEM((6 * BLK, BLK), f32),
+            pltpu.VMEM((3, 6 * BLK // 4, BLK), f32),
+            pltpu.VMEM((3, 6 * BLK // 16, BLK), f32),
+            pltpu.VMEM((3, 6 * BLK // 64, BLK), f32),
+            pltpu.VMEM((BLK, 2 * HEAD_DIM), f32),
+            pltpu.VMEM((3, BLK // 4, 2 * HEAD_DIM), f32),
+            pltpu.VMEM((3, BLK // 16, 2 * HEAD_DIM), f32),
+            pltpu.SemaphoreType.DMA((48,)),
+            pltpu.SemaphoreType.DMA((48,)),
+        ],
+        name="sum_grams",
+        compiler_params=pltpu.CompilerParams(
+            collective_id=0, has_side_effects=True, vmem_limit_bytes=48 * 2**20
+        ),
+    )(g_ffn, g_heads, m_ffn, m_heads, small)
+
+
+def chain_kernel(gram_in, hgram_in, x_in, xh_in, x_out, xh_out, gram, high, low, next_high, next_low, iterate, hgram):
+    def tile(i):
+        return slice(i * BLK, (i + 1) * BLK)
+
+    eye = (
+        lax.broadcasted_iota(jnp.int32, (BLK, BLK), 0)
+        == lax.broadcasted_iota(jnp.int32, (BLK, BLK), 1)
+    ).astype(jnp.float32)
+    trace = jnp.zeros((1, 1), jnp.float32)
+    for number, (i, j) in enumerate(UPPER):
+        block = gram_in[tile(number), :]
+        gram[tile(i), tile(j)] = block
+        if i == j:
+            trace = trace + jnp.sum(block * eye, axis=(0, 1), keepdims=True)
+        else:
+            gram[tile(j), tile(i)] = block.T
+    scale = 1.0 / (jnp.sqrt(trace) + NS_EPS)
+    gram[...] = gram[...] * (scale * scale)
+    iterate[...] = x_in[...] * scale
+    cols = xh_in.shape[2]
+    h_rows = lax.broadcasted_iota(jnp.int32, (cols, cols), 0)
+    h_cols = lax.broadcasted_iota(jnp.int32, (cols, cols), 1)
+    same = h_rows // HEAD_DIM == h_cols // HEAD_DIM
+    h_eye = (h_rows == h_cols).astype(jnp.float32)
+    for kind in range(2):
+        folded = hgram_in[:cols, kind * HEAD_DIM : (kind + 1) * HEAD_DIM]
+        full = jnp.where(same, jnp.concatenate([folded] * (cols // HEAD_DIM), axis=1), 0.0)
+        on_diagonal = full * h_eye
+        by_column = jnp.sum(on_diagonal, axis=0, keepdims=True)
+        by_row = jnp.sum(on_diagonal, axis=1, keepdims=True)
+        trace_row = jnp.sum(jnp.where(same, by_column, 0.0), axis=1, keepdims=True)
+        trace_column = jnp.sum(jnp.where(same, by_row, 0.0), axis=0, keepdims=True)
+        scale_column = 1.0 / (jnp.sqrt(trace_column) + NS_EPS)
+        scale_row = 1.0 / (jnp.sqrt(trace_row) + NS_EPS)
+        hgram[kind] = full * scale_row * scale_column
+        xh_out[kind] = xh_in[kind] * scale_column
+
+    def sweep_heads(last):
+        for kind in range(2):
+            current = hgram[kind]
+            pieces = split(current)
+            poly = COEF_A * h_eye + COEF_B * current + COEF_C * product(pieces, pieces)
+            poly_pieces = split(poly)
+            xh_out[kind] = product(split(xh_out[kind]), poly_pieces)
+            if not last:
+                hgram[kind] = product(split(product(pieces, poly_pieces)), poly_pieces)
+
+    def sweep(last):
+        current = gram[...]
+        high[...], low[...] = split(current)
+        for i in range(3):
+            squared = product((high[tile(i), :], low[tile(i), :]), (high[...], low[...]))
+            poly = COEF_B * gram[tile(i), :] + COEF_C * squared
+            next_high[tile(i), :], next_low[tile(i), :] = split(
+                poly
+                + COEF_A
+                * jnp.concatenate(
+                    [eye if k == i else jnp.zeros((BLK, BLK), jnp.float32) for k in range(3)], axis=1
+                )
+            )
+        factor = (next_high[...], next_low[...])
+        iterate[...] = product(split(iterate[...]), factor)
+        if not last:
+            for i in range(3):
+                half = product((high[tile(i), :], low[tile(i), :]), factor)
+                gram[tile(i), :] = product(split(half), factor)
+        sweep_heads(last)
+
+    def body(_, carry):
+        sweep(False)
+        return carry
+
+    lax.fori_loop(0, NS_ITERS - 1, body, 0)
+    sweep(True)
+    x_out[...] = iterate[...]
+
+
+def chain(gram, hgram, iterate, head_iterate):
+    f32, b16 = jnp.float32, jnp.bfloat16
+    cols = head_iterate.shape[2]
+    vmem = pl.BlockSpec(memory_space=pltpu.VMEM)
+    return pl.pallas_call(
+        chain_kernel,
+        out_shape=[
+            jax.ShapeDtypeStruct(iterate.shape, f32),
+            jax.ShapeDtypeStruct(head_iterate.shape, f32),
+        ],
+        in_specs=[vmem] * 4,
+        out_specs=[vmem] * 2,
+        scratch_shapes=[
+            pltpu.VMEM((D, D), f32),
+            pltpu.VMEM((D, D), b16),
+            pltpu.VMEM((D, D), b16),
+            pltpu.VMEM((D, D), b16),
+            pltpu.VMEM((D, D), b16),
+            pltpu.VMEM(iterate.shape, f32),
+            pltpu.VMEM((2, cols, cols), f32),
+        ],
+        name="chain",
+        compiler_params=pltpu.CompilerParams(vmem_limit_bytes=48 * 2**20),
+    )(gram, hgram, iterate, head_iterate)
+
+
+def swap_kernel(o_ffn, o_heads, ffn_out, heads_out, send_sem, recv_sem):
+    x, y, z, core = place()
+    sems = (send_sem, recv_sem)
+    sibling = device(x, y, z, 1 - core)
+    greet([sibling])
+    copies = [
+        send(o_ffn.at[rows((1 - core) * SUB, SUB)], ffn_out.at[core], sems, 0, sibling)
+    ]
+    for kind in range(2):
+        copies.append(
+            send(
+                o_heads.at[kind, rows((1 - core) * SUB, SUB)],
+                heads_out.at[2 * core + kind],
+                sems,
+                1 + kind,
+                sibling,
+            )
+        )
+    ffn_out[core] = o_ffn[rows(core * SUB, SUB), :]
+    for kind in range(2):
+        heads_out[2 * core + kind] = o_heads[kind, rows(core * SUB, SUB), :]
+    for copy in copies:
+        copy.wait()
+
+
+def swap(o_ffn, o_heads):
+    vmem = pl.BlockSpec(memory_space=pltpu.VMEM)
+    cols = o_heads.shape[2]
+    return pl.pallas_call(
+        swap_kernel,
+        out_shape=[
+            jax.ShapeDtypeStruct((2, SUB, D), jnp.float32),
+            jax.ShapeDtypeStruct((4, SUB, cols), jnp.float32),
+        ],
+        in_specs=[vmem] * 2,
+        out_specs=[vmem] * 2,
+        scratch_shapes=[pltpu.SemaphoreType.DMA((3,)), pltpu.SemaphoreType.DMA((3,))],
+        name="swap",
+        compiler_params=pltpu.CompilerParams(collective_id=1, has_side_effects=True),
+    )(o_ffn, o_heads)
 
 
 def adam_step(weight, gradient, moment_one, moment_two):
@@ -325,15 +702,21 @@
     conv_placed = lax.dynamic_update_slice_in_dim(
         jnp.zeros(conv.shape, jnp.float32), kernel_grad, head_at * cols_here, 2
     )
-    squares = (
-        jnp.sum(qkv_part * qkv_part)
-        + jnp.sum(out_part * out_part)
-        + jnp.sum(ffn_part_grad * ffn_part_grad)
-    )
-    gain_sum, conv_sum, square_sum = lax.psum(
-        (jnp.stack([gain_one_grad, gain_two_grad]), conv_placed, squares), ("head", "dp")
-    )
-    grad_norm = jnp.sqrt(square_sum + jnp.sum(gain_sum * gain_sum) + jnp.sum(conv_sum * conv_sum))
+    small = jnp.concatenate(
+        [
+            jnp.stack([gain_one_grad, gain_two_grad]),
+            conv_placed.reshape(KW * 3, D),
+            jnp.zeros((5, D), jnp.float32),
+        ]
+    )
+    heads_grad = jnp.concatenate([qkv_part, out_part.T[None]])
+    heads_mom = jnp.concatenate([mom_qkv, mom_out.T[None]])
+    small_sum, gram, hgram, iterate, head_iterate = sum_over_devices(
+        ffn_part_grad, heads_grad, mom_ffn, heads_mom, small
+    )
+    gain_sum = small_sum[:2]
+    conv_sum = small_sum[2:11].reshape(conv.shape)
+    grad_norm = jnp.sqrt(jnp.sum(small_sum[:11] * small_sum[:11]) + jnp.sum(small_sum[11]))
     factor = CLIP_NORM / jnp.maximum(grad_norm, CLIP_NORM)
     grad_gains = gain_sum * factor
     grad_conv = conv_sum * factor
@@ -343,38 +726,10 @@
     new_mom_qkv = MOMENTUM * mom_qkv + grad_qkv
     new_mom_out = MOMENTUM * mom_out + grad_out
     new_mom_ffn = MOMENTUM * mom_ffn + grad_ffn
-    shard_rows = w_qkv.shape[1]
-    head_iter = jnp.concatenate(
-        [
-            new_mom_qkv.reshape(3, shard_rows, heads_local, HEAD_DIM).transpose(0, 2, 1, 3),
-            new_mom_out.reshape(heads_local, HEAD_DIM, shard_rows).transpose(0, 2, 1)[None],
-        ],
-        0,
-    )
-    ffn_iter = new_mom_ffn
-    head_offset = head_at * heads_local
-    for sweep in range(NS_ITERS):
-        local_ffn = jnp.einsum("knd,kne->kde", ffn_iter, ffn_iter, precision=PRECISE)
-        local_heads = jnp.einsum("kgnd,kgne->kgde", head_iter, head_iter, precision=PRECISE)
-        placed = lax.dynamic_update_slice_in_dim(
-            jnp.zeros((4, HEADS, HEAD_DIM, HEAD_DIM), jnp.float32), local_heads, head_offset, 1
-        )
-        gram_ffn, gram_placed = lax.psum((local_ffn, placed), ("head", "dp"))
-        gram_heads = lax.dynamic_slice_in_dim(gram_placed, head_offset, heads_local, 1)
-        if sweep == 0:
-            ffn_scale = 1.0 / (jnp.sqrt(jnp.trace(gram_ffn, axis1=1, axis2=2)) + NS_EPS)
-            head_scale = 1.0 / (jnp.sqrt(jnp.trace(gram_heads, axis1=2, axis2=3)) + NS_EPS)
-            ffn_iter = ffn_iter * ffn_scale[:, None, None]
-            gram_ffn = gram_ffn * jnp.square(ffn_scale)[:, None, None]
-            head_iter = head_iter * head_scale[:, :, None, None]
-            gram_heads = gram_heads * jnp.square(head_scale)[:, :, None, None]
-        ffn_iter = ns_update(ffn_iter, gram_ffn)
-        head_iter = ns_update(head_iter, gram_heads)
-    qkv_orth = head_iter[:3].transpose(0, 2, 1, 3).reshape(3, shard_rows, cols_here)
-    out_orth = head_iter[3].transpose(0, 2, 1).reshape(cols_here, shard_rows)
-    new_qkv = w_qkv - RATE_IN * math.sqrt(D) * qkv_orth
-    new_out = w_out - RATE_OUT * math.sqrt(D) * out_orth
-    new_ffn = ffn_weights - RATE_IN * math.sqrt(max(FF, D)) * ffn_iter
+    ffn_orth, heads_orth = swap(*chain(gram, hgram, iterate, head_iterate))
+    new_qkv = w_qkv - RATE_IN * math.sqrt(D) * heads_orth[:3]
+    new_out = w_out - RATE_OUT * math.sqrt(D) * heads_orth[3].T
+    new_ffn = ffn_weights - RATE_IN * math.sqrt(max(FF, D)) * ffn_orth
     new_gain_first, new_gain_second, new_gains = adam_step(
         gains, grad_gains, gain_first, gain_second
     )

time: 1630 us -> 755 us (0.46)
  waiting for transfers between devices: 1130 us -> 358 us
  matrix products: 272 us -> 140 us
  Pallas kernels: 0 us -> 117 us
  blocking collectives: 120 us -> 54.5 us
    psum x5 -> x0, waiting for transfers between devices: 774 us -> none  [per_device(): gram_ffn, gram_placed = lax.psum((local_ffn, placed), ('head', 'dp'))]
    dot_general x30 -> x0, matrix products: 131 us -> none  [the longest x10 81.6 us: ns_update(): jnp.einsum('...de,...ef->...df', gram_matrix, gram_matrix, precision=PREC...]
    pallas_call x0 -> x3, Pallas kernels: none -> 117 us  [the longest x1 62.5 us: sum_over_devices(): pl.pallas_call(sum_kernel, out_shape=[jax.ShapeDtypeStruct((16, D), f32),...]
    psum x1 -> x0, blocking collectives: 66 us -> none  [per_device(): lax.psum((jnp.stack([gain_one_grad, gain_two_grad]), conv_placed, squares...]
    unnamed x19 -> x14, waiting for transfers between devices: 90.7 us -> 89.3 us
  transfers between devices with their start and end apart: 17 -> 12, of which waited for: 15 -> 10; matrix products, arithmetic and copies ran while one was open for 9% -> 19% of each run, Pallas kernels for 0% -> 0%
where the time goes in v2:
time: 755 us; the launch traced here: 751 us
  waiting for transfers between devices  358 us (47%)
  matrix products  140 us (19%)
  Pallas kernels  117 us (15%)
  blocking collectives  54.5 us (7%)
  other arithmetic  40.4 us (5%)
  between operations  20.1 us (3%)
  local copies, waits for them, and re-layouts  19.8 us (3%)
    unnamed x14, waiting for transfers between devices  89.3 us
    reduce_scatter x1, waiting for transfers between devices, per_device(): lax.psum_scatter(out_grad.astype(jnp.bfloat16), 'dp', scatter_dimension=1...  75.2 us
    pallas_call x1, Pallas kernels, sum_over_devices(): pl.pallas_call(sum_kernel, out_shape=[jax.ShapeDtypeStruct((16, D), f32),...  62.5 us
    pallas_call x1, Pallas kernels, chain(): pl.pallas_call(chain_kernel, out_shape=[jax.ShapeDtypeStruct(iterate.shap...  45 us
    reduce_scatter x1, waiting for transfers between devices, per_device(): lax.psum_scatter(projection_portion, 'head', scatter_dimension=1, tiled=T...  35.9 us
    dot_general x2, matrix products, attend_back(): jnp.einsum('hqk,qhd->khd', score_grad, query_rows, preferred_element_type...  35.5 us
    reduce_scatter x1, waiting for transfers between devices, per_device(): lax.psum_scatter(grad_normed_part, 'head', scatter_dimension=1, tiled=True)  33.7 us
    dot_general x2, matrix products, attend_back(): jnp.einsum('hqk,khd->qhd', score_grad, keys_all, preferred_element_type=j...  32.5 us
  transfers between devices with their start and end apart: 12, of which 10 were waited for; matrix products, arithmetic and copies ran while one was open for 19% of the time, Pallas kernels for 0%

profile of v2, /device:TPU:1, one launch (start us, length us, event | category | flops | bytes accessed | tf_op | source)
XLA Modules:
  0.0 750.9 jit_solution(15102322905502102983)
XLA Ops:
  8.1 1.2 fusion.130
  10.0 1.9 fusion.127
  14.3 27.5 %all_gather.23 = bf16[192,768]{0,1:T(8,128)(2,1)S(1)} all-gather(bf16[192,24]{0,1:T(8,128)(2,1)S(1)} %convert_element_type.168), channel_id=1, replica_groups=mesh['head'=4,'dp'=32] {'dp'}, dimensions={1}, use_global_device_ids=true | all-gather | bytes 304128 | tf_op jit(solution)/shard_map/all_gather | solution.py:601
  41.8 0.9 dynamic-slice_bitcast_fusion.2
  42.8 27.0 %all_gather.22 = bf16[3,768,192]{2,1,0:T(8,128)(2,1)} all-gather(bf16[3,24,192]{2,1,0:T(8,128)(2,1)S(1)} %convert_element_type.163), channel_id=1, replica_groups=mesh['head'=4,'dp'=32] {'dp'}, dimensions={1}, use_global_device_ids=true | all-gather | bytes 912384 | tf_op jit(solution)/shard_map/all_gather | solution.py:600
  69.8 1.5 fusion.35
  71.2 2.9 convolution_bitcast_fusion.2
  74.1 1.7 add_convert_fusion
  76.7 7.0 fusion.163
  83.6 6.7 fusion.164
  90.3 4.1 fusion.115
  94.9 1.2 fusion.112
  96.8 2.7 convolution_bitcast_fusion.1
  100.3 35.9 %reduce-scatter.10.cloned.1.call-done = f32[1,256,768]{2,1,0:T(8,128)} async-done(((f32[1,1024,768]{2,1,0:T(8,128)}), f32[1,256,768]{2,1,0:T(8,128)}) %reduce-scatter.10.cloned.1.call-update) | async-done | bytes 786448 | tf_op jit(solution)/shard_map/reduce_scatter | solution.py:624
  136.1 1.4 multiply_reduce_fusion.7
  139.6 1.9 fusion.131
  141.5 4.2 all-gather.10.cloned.1.call-done
  145.8 27.3 %all-gather.8.cloned.1.call-done = bf16[1,1024,768]{2,1,0:T(8,128)(2,1)} async-done(((bf16[1,256,768]{2,1,0:T(8,128)(2,1)}), bf16[1,1024,768]{2,1,0:T(8,128)(2,1)}) %all-gather.8.cloned.1.call-update) | async-done | bytes 1572880 | tf_op jit(solution)/shard_map/all_gather | solution.py:629
  173.0 4.8 fusion.46
  177.8 23.7 %all-gather.12.cloned.1.call-done = bf16[1,1024,768]{2,1,0:T(8,128)(2,1)} async-done(((bf16[1,256,768]{2,1,0:T(8,128)(2,1)}), bf16[1,1024,768]{2,1,0:T(8,128)(2,1)}) %all-gather.12.cloned.1.call-update) | async-done | bytes 1572880 | tf_op jit(solution)/shard_map/all_gather | solution.py:635
  201.6 4.3 multiply_convert_fusion.2
  205.9 1.2 copy-done.39
  207.1 3.0 convolution_bitcast_fusion
  210.2 4.8 fusion.66
  215.1 33.7 %reduce-scatter.14.cloned.1.call-done = f32[1,256,768]{2,1,0:T(8,128)} async-done(((f32[1,1024,768]{2,1,0:T(8,128)}), f32[1,256,768]{2,1,0:T(8,128)}) %reduce-scatter.14.cloned.1.call-update) | async-done | bytes 786448 | tf_op jit(solution)/shard_map/reduce_scatter | solution.py:639
  248.8 2.0 multiply_reduce_fusion.5
  251.4 24.0 %reduce-scatter.12.cloned.1.call-done = bf16[1,256,768]{2,1,0:T(8,128)(2,1)} async-done(((bf16[1,1024,768]{2,1,0:T(8,128)(2,1)}), bf16[1,256,768]{2,1,0:T(8,128)(2,1)}) %reduce-scatter.12.cloned.1.call-update) | async-done | bytes 393232 | tf_op jit(solution)/shard_map/reduce_scatter | solution.py:631
  275.4 3.0 fusion.159
  278.5 3.5 fusion.73
  282.0 1.5 fusion.70
  283.7 2.4 copy.37
  286.2 1.9 copy.41
  288.2 17.3 %all-gather.14.cloned.1.call-done = bf16[1,1024,768]{2,1,0:T(8,128)(2,1)} async-done(((bf16[1,256,768]{2,1,0:T(8,128)(2,1)}), bf16[1,1024,768]{2,1,0:T(8,128)(2,1)}) %all-gather.14.cloned.1.call-update) | async-done | bytes 1572880 | tf_op jit(solution)/shard_map/all_gather | solution.py:642
  305.5 2.1 fusion.97
  307.7 3.6 fusion.165
  311.3 3.6 fusion.166
  314.9 16.3 %fusion.118 = bf16[512,3,64]{0,2,1:T(8,128)(2,1)} fusion(bf16[1024,3,64]{0,2,1:T(8,128)(2,1)S(1)} %bitcast.181, f32[3,512,1024]{2,1,0:T(8,128)} %fusion.165, f32[3,512,1024]{2,1,0:T(8,128)} %get-tuple-element.136, f32[3,512]{1,0:T(4,128)} %get-tuple-element.135), kind=kOutput, calls=%fused_computation.106 | convolution fusion | flops 212437504 | bytes 13178880 | tf_op jit(solution)/shard_map/while/body/eval_jaxpr/hqk,khd->qhd/dot_general | solution.py:123
  331.2 16.2 %fusion.121 = bf16[512,3,64]{0,2,1:T(8,128)(2,1)} fusion(bf16[1024,3,64]{0,2,1:T(8,128)(2,1)S(1)} %bitcast.182, f32[3,512,1024]{2,1,0:T(8,128)} %fusion.166, f32[3,512,1024]{2,1,0:T(8,128)} %get-tuple-element.134, f32[3,512]{1,0:T(4,128)} %get-tuple-element.133), kind=kOutput, calls=%fused_computation.107 | convolution fusion | flops 212437504 | bytes 13178880 | tf_op jit(solution)/shard_map/while/body/eval_jaxpr/hqk,khd->qhd/dot_general | solution.py:123
  347.4 1.1 pad_maximum_fusion.3
  348.5 18.2 %fusion.17 = f32[3,64,1024]{2,1,0:T(8,128)} fusion(bf16[512,3,64]{0,2,1:T(8,128)(2,1)} %bitcast.190, f32[3,512,1024]{2,1,0:T(8,128)} %fusion.165, f32[3,512,1024]{2,1,0:T(8,128)} %get-tuple-element.136, f32[3,512]{1,0:T(4,128)} %get-tuple-element.135), kind=kOutput, calls=%fused_computation.25 | convolution fusion | flops 212339200 | bytes 13572096 | tf_op jit(solution)/shard_map/while/body/eval_jaxpr/hqk,qhd->khd/dot_general | solution.py:125
  366.7 17.3 %fusion.85 = bf16[3,64,1024]{2,1,0:T(8,128)(2,1)S(1)} fusion(f32[3,64,1024]{2,1,0:T(8,128)} %fusion.17, bf16[512,3,64]{0,2,1:T(8,128)(2,1)} %bitcast.188, f32[3,512,1024]{2,1,0:T(8,128)} %fusion.166, f32[3,512,1024]{2,1,0:T(8,128)} %get-tuple-element.134, f32[3,512]{1,0:T(4,128)} %get-tuple-element.133), kind=kOutput, calls=%fused_computation.85 | convolution fusion | flops 212732416 | bytes 13965312 | tf_op jit(solution)/shard_map/while/body/eval_jaxpr/hqk,qhd->khd/dot_general | solution.py:125
  384.0 3.7 fusion.51
  387.8 3.6 fusion.88
  392.3 1.8 fusion.33
  394.1 1.0 copy-done.11
  395.1 2.0 fusion.76
  397.1 2.5 copy.36
  399.7 2.9 fusion.94
  402.7 4.3 fusion.65
  409.0 1.6 reshape.382
  412.0 3.2 multiply_reduce_fusion.4
  415.6 89.1 %all-reduce.7.cloned.1.call-done = bf16[3,768,192]{2,1,0:T(8,128)(2,1)} async-done(((bf16[3,768,192]{2,1,0:T(8,128)(2,1)}), bf16[3,768,192]{2,1,0:T(8,128)(2,1)}) %all-reduce.7.cloned.1.call-update) | async-done | bytes 884752
  505.4 75.2 %reduce-scatter.18.cloned.1.call-done = bf16[192,24]{0,1:T(8,128)(2,1)} async-done(((bf16[192,768]{0,1:T(8,128)(2,1)}), bf16[192,24]{0,1:T(8,128)(2,1)}) %reduce-scatter.18.cloned.1.call-update) | async-done | bytes 9232 | tf_op jit(solution)/shard_map/reduce_scatter | solution.py:695
  581.3 27.7 %reduce-scatter.16.cloned.1.call-done = bf16[1,256,768]{2,1,0:T(8,128)(2,1)} async-done(((bf16[1,1024,768]{2,1,0:T(8,128)(2,1)}), bf16[1,256,768]{2,1,0:T(8,128)(2,1)}) %reduce-scatter.16.cloned.1.call-update) | async-done | bytes 393232 | tf_op jit(solution)/shard_map/reduce_scatter | solution.py:686
  609.0 1.4 fusion.129
  611.2 62.5 %sum_grams.1 = (f32[16,768]{1,0:T(8,128)S(1)}, f32[1536,256]{1,0:T(8,128)S(1)}, f32[256,128]{1,0:T(8,128)S(1)}, f32[48,768]{1,0:T(8,128)S(1)}, f32[2,48,192]{2,1,0:T(8,128)S(1)}) custom-call(f32[2,24,768]{2,1,0:T(8,128)S(1)} %copy_convert_fusion.g_ffn, f32[4,24,192]{2,1,0:T(8,128)S(1)} %pad_maximum_fusion.4.g_heads, f32[2,24,768]{2,1,0:T(8,128)S(1)} %copy-done, ...), custom_call_target="tpu_custom_call" | custom-call | tf_op jit(solution)/shard_map/sum_grams/pallas_call | solution.py:380
  676.4 45.0 %chain.1 = (f32[48,768]{1,0:T(8,128)S(1)}, f32[2,48,192]{2,1,0:T(8,128)S(1)}) custom-call(f32[1536,256]{1,0:T(8,128)S(1)} %get-tuple-element.87.gram_in, f32[256,128]{1,0:T(8,128)S(1)} %get-tuple-element.88.hgram_in, f32[48,768]{1,0:T(8,128)S(1)} %get-tuple-element.89.x_in, f32[2,48,192]{2,1,0:T(8,128)S(1)} %get-tuple-element.90.xh_in), custom_call_target="tpu_custom_call" | custom-call | tf_op jit(solution)/shard_map/chain/pallas_call | solution.py:498
  722.8 9.7 %swap.1 = (f32[2,24,768]{2,1,0:T(8,128)}, f32[4,24,192]{2,1,0:T(8,128)}) custom-call(f32[48,768]{1,0:T(8,128)} %copy-done.1, f32[2,48,192]{2,1,0:T(8,128)} %copy-done.2), custom_call_target="tpu_custom_call" | custom-call | tf_op jit(solution)/shard_map/swap/pallas_call | solution.py:548
  732.5 1.8 multiply_add_fusion.1
  734.3 1.3 multiply_subtract_fusion.3
  735.6 1.5 multiply_subtract_fusion.2
  737.1 1.7 multiply_add_fusion.2
  738.8 1.4 multiply_add_fusion.4
  740.2 2.3 fusion.126
  (147 shorter events, 17.6 us)
Async XLA Ops:
  8.0 63.2 %all-gather.6.cloned.1.call-start = ((), (), s32[]{:S(2)}) async-start(), calls=%async_computation.6 | async-start | bytes 1966080 | tf_op jit(solution)/shard_map/all_gather | solution.py:606
  9.2 5.1 copy-start.29
  12.0 124.1 %reduce-scatter.10.cloned.1.call-start = ((), (), s32[]{:S(2)}) async-start(), calls=%async_computation.7 | async-start | bytes 3932160 | tf_op jit(solution)/shard_map/reduce_scatter | solution.py:624
  41.8 54.4 %copy-start.4 = (bf16[192,768]{0,1:T(8,128)(2,1)}, bf16[192,768]{0,1:T(8,128)(2,1)S(1)}, u32[]{:S(2)}) copy-start(bf16[192,768]{0,1:T(8,128)(2,1)S(1)} %all_gather.23) | copy-start | bytes 884740
  42.7 31.3 %copy-start.26 = (f32[3,192]{1,0:T(4,128)}, f32[3,192]{1,0:T(4,128)S(1)}, u32[]{:S(2)}) copy-start(f32[3,192]{1,0:T(4,128)S(1)} %get-tuple-element.130) | copy-start | bytes 6916
  76.6 7.0 copy-start.16
  76.6 17.8 %copy-start.6 = (bf16[1,1,1024,192]{2,3,0,1:T(8,128)(2,1)}, bf16[1,1,1024,192]{2,3,0,1:T(8,128)(2,1)S(1)}, u32[]{:S(2)}) copy-start(bf16[1,1,1024,192]{2,3,0,1:T(8,128)(2,1)S(1)} %get-tuple-element.124) | copy-start | bytes 1179652
  90.3 4.6 copy-start.40
  90.3 4.6 copy-start.41
  94.4 1.7 copy-start.19
  96.1 0.7 copy-start.21
  96.8 2.7 copy-start.15
  99.5 36.7 %copy-start.3 = (bf16[1,256,768]{2,1,0:T(8,128)(2,1)S(1)}, bf16[1,256,768]{2,1,0:T(8,128)(2,1)}, u32[]{:S(2)}) copy-start(bf16[1,256,768]{2,1,0:T(8,128)(2,1)} %param.15) | copy-start | bytes 1179652
  99.5 46.3 %all-gather.10.cloned.1.call-start = ((), (), s32[]{:S(2)}) async-start(), calls=%async_computation.9 | async-start | bytes 2433024 | tf_op jit(solution)/shard_map/all_gather | solution.py:602
  100.2 72.8 %all-gather.8.cloned.1.call-start = ((), (), s32[]{:S(2)}) async-start(), calls=%async_computation.8 | async-start | bytes 1966080 | tf_op jit(solution)/shard_map/all_gather | solution.py:629
  137.5 0.6 copy-start.32
  139.0 62.6 %all-gather.12.cloned.1.call-start = ((), (), s32[]{:S(2)}) async-start(), calls=%async_computation.11 | async-start | bytes 1966080 | tf_op jit(solution)/shard_map/all_gather | solution.py:635
  139.0 0.6 copy-start.33
  141.5 107.3 %reduce-scatter.14.cloned.1.call-start = ((), (), s32[]{:S(2)}) async-start(), calls=%async_computation.12 | async-start | bytes 3932160 | tf_op jit(solution)/shard_map/reduce_scatter | solution.py:639
  201.6 5.5 copy-start.34
  205.9 1.2 copy-start.39
  210.2 65.2 %reduce-scatter.12.cloned.1.call-start = ((), (), s32[]{:S(2)}) async-start(), calls=%async_computation.10 | async-start | bytes 1966080 | tf_op jit(solution)/shard_map/reduce_scatter | solution.py:631
  215.0 90.5 %all-gather.14.cloned.1.call-start = ((), (), s32[]{:S(2)}) async-start(), calls=%async_computation.13 | async-start | bytes 1966080 | tf_op jit(solution)/shard_map/all_gather | solution.py:642
  278.4 130.6 %reduce-scatter.20.cloned.1.call-start = ((), (), s32[]{:S(2)}) async-start(), calls=%async_computation.16 | async-start | bytes 2433024
  278.5 3.5 copy-start.36
  278.5 3.5 copy-start.38
  286.2 19.3 %copy-start.5 = (bf16[192,768]{0,1:T(8,128)(2,1)S(1)}, bf16[192,768]{0,1:T(8,128)(2,1)}, u32[]{:S(2)}) copy-start(bf16[192,768]{0,1:T(8,128)(2,1)} %copy-done.4) | copy-start | bytes 884740
  288.1 19.6 %copy-start.7 = (bf16[1,1,1024,192]{2,3,0,1:T(8,128)(2,1)S(1)}, bf16[1,1,1024,192]{2,3,0,1:T(8,128)(2,1)}, u32[]{:S(2)}) copy-start(bf16[1,1,1024,192]{2,3,0,1:T(8,128)(2,1)} %copy-done.6) | copy-start | bytes 1179652
  288.1 216.6 %all-reduce.7.cloned.1.call-start = ((), (), s32[]{:S(2)}) async-start(), calls=%async_computation.17 | async-start | bytes 2359296
  307.6 3.7 copy-start.12
  307.6 3.7 copy-start.14
  311.3 3.6 copy-start.17
  384.0 7.4 copy-start.8
  384.0 3.8 copy-start.13
  384.0 3.8 copy-start.42
  391.4 0.8 copy-start.9
  391.4 0.9 copy-start.27
  392.3 2.8 copy-start.35
  394.1 1.0 copy-start.11
  397.1 2.6 copy-start.20
  397.1 2.6 copy-start.22
  399.6 181.0 %reduce-scatter.18.cloned.1.call-start = ((), (), s32[]{:S(2)}) async-start(), calls=%async_computation.15 | async-start | bytes 405504 | tf_op jit(solution)/shard_map/reduce_scatter | solution.py:695
  402.6 4.4 copy-start.37
  402.7 6.3 copy-start.18
  402.7 6.2 copy-start.24
  402.7 8.8 %copy-start.31 = (f32[768]{0:T(1024)S(1)}, f32[768]{0:T(1024)}, u32[]{:S(2)}) copy-start(f32[768]{0:T(1024)} %get-tuple-element.98) | copy-start | bytes 9220
  402.7 206.3 %reduce-scatter.16.cloned.1.call-start = ((), (), s32[]{:S(2)}) async-start(), calls=%async_computation.14 | async-start | bytes 1966080 | tf_op jit(solution)/shard_map/reduce_scatter | solution.py:686
  407.1 202.0 %copy-start.30 = (f32[256]{0:T(256)S(1)}, f32[256]{0:T(256)}, u32[]{:S(2)}) copy-start(f32[256]{0:T(256)} %copy-done.29) | copy-start | bytes 3076
  408.9 202.3 %copy-start = (f32[2,24,768]{2,1,0:T(8,128)S(1)}, f32[2,24,768]{2,1,0:T(8,128)}, u32[]{:S(2)}) copy-start(f32[2,24,768]{2,1,0:T(8,128)} %m_ffn.1) | copy-start | bytes 442372
  415.6 318.7 %copy-start.28 = (f32[2,768]{1,0:T(2,128)S(1)}, f32[2,768]{1,0:T(2,128)}, u32[]{:S(2)}) copy-start(f32[2,768]{1,0:T(2,128)} %param.18) | copy-start | bytes 18436
  581.3 157.4 %copy-start.25 = (bf16[192,24]{0,1:T(8,128)(2,1)S(1)}, bf16[192,24]{0,1:T(8,128)(2,1)}, u32[]{:S(2)}) copy-start(bf16[192,24]{0,1:T(8,128)(2,1)} %reduce-scatter.18.cloned.1.call-done) | copy-start | bytes 27652
  610.4 129.8 %copy-start.10 = (bf16[1,256,768]{2,1,0:T(8,128)(2,1)S(1)}, bf16[1,256,768]{2,1,0:T(8,128)(2,1)}, u32[]{:S(2)}) copy-start(bf16[1,256,768]{2,1,0:T(8,128)(2,1)} %reduce-scatter.16.cloned.1.call-done) | copy-start | bytes 1179652
  676.4 66.0 %copy-start.23 = (f32[3,3,768]{2,1,0:T(4,128)}, f32[3,3,768]{2,1,0:T(4,128)S(1)}, u32[]{:S(2)}) copy-start(f32[3,3,768]{2,1,0:T(4,128)S(1)} %mul.424) | copy-start | bytes 82948
  721.5 0.7 copy-start.1
  722.1 0.6 copy-start.2
Sparse Core Ops, SparseCore 0:
  12.1 29.7 all-gather.5
  99.6 36.4 reduce-scatter.9
  210.3 38.4 reduce-scatter.13
  251.0 24.3 reduce-scatter.11
Sparse Core Ops, SparseCore 1:
  102.9 42.8 all-gather.9
  147.9 25.1 all-gather.7
  175.1 26.4 all-gather.11
  278.5 27.0 all-gather.13
  309.1 78.3 reduce-scatter.19
  399.7 104.9 all-reduce.6
  508.4 72.1 reduce-scatter.17
  583.0 25.9 reduce-scatter.15
